TPU v7x, 256 devices: a whole 4x4x8 slice. The times are simulated.
256 devices in a mesh: imp: 64 (over y, z, core), ad: 4 (over x).
Axes of the slice: x: 4, y: 4, z: 8, core: 2. Of those that a mesh axis runs over, the one named last changes fastest.
Arguments:
- imp_vectors: bfloat16 [65536, 128], P('imp'), may hold values from -32 to 32
- ad_vectors: bfloat16 [1572864, 128], P(('imp', 'ad')), may hold values from -1 to 1
- spend_limits: float32 [1572864], P(('imp', 'ad')), may hold values from 0.005 to 0.05
- targets: int32 [64, 4, 32], P('imp', 'ad'), may hold values from 0 to 3071, as said below
Outputs:
- pacing: float32 [1572864], P(('imp', 'ad'))
- prices: float32 [65536], P('imp')
Inputs may be any that keep to these rules, and one draw needn't show every extreme that they name: No block appears twice in one list targets[i, a, :]; at most 2 entries of one list share the owner q // 48, and in each column a some owner gets exactly 2 entries from every impression block.
All inputs are finite; a program needn't handle non-finite values.
Results may differ from a plain program's by a relative error of at most 0.0003.
Values may be sent and summed in bfloat16 or wider, within the bound.
No kernel may reach another device: no remote copies, remote signals or barrier semaphores. Data moves between devices by JAX's collectives and lax.ppermute only.
A program may use at most 128 MiB of HBM per device.

v0:
```python
import jax
import jax.numpy as jnp
from jax import lax
from jax.sharding import PartitionSpec as P

BLOCK = 128
ROUNDS = 4


softness_level = 0.5
util_floor = 0.01
pacing_cap = 3.0


def per_device(imp_vectors, ad_vectors, spend_limits, targets):
    owner_total = lax.axis_size("imp")
    emb_width = imp_vectors.shape[1]
    own_blocks = ad_vectors.shape[0] // BLOCK
    wanted = targets.reshape(-1)
    list_size = wanted.shape[0]
    capacity = max(2, (2 * list_size + owner_total - 1) // owner_total)
    slot_total = owner_total * capacity
    owner_of = wanted // own_blocks
    local_of = wanted % own_blocks
    slot_order = jnp.arange(list_size, dtype=jnp.int32)
    earlier = (owner_of[:, None] == owner_of[None, :]) & (slot_order[None, :] < slot_order[:, None])
    rank_of = jnp.sum(earlier.astype(jnp.int32), axis=1)
    position = owner_of * capacity + rank_of
    placed = position[None, :] == jnp.arange(slot_total, dtype=jnp.int32)[:, None]
    requests = jnp.where(
        jnp.any(placed, axis=1), jnp.sum(jnp.where(placed, local_of[None, :], 0), axis=1), -1
    )
    asked = lax.all_to_all(
        requests.reshape(owner_total, capacity), "imp", split_axis=0, concat_axis=0, tiled=True
    ).reshape(slot_total)
    source = jnp.maximum(asked, 0)
    returned = (asked[None, :] == jnp.arange(own_blocks, dtype=jnp.int32)[:, None]).astype(
        jnp.float32
    )
    placed_float = placed.astype(jnp.float32)
    own_vectors = ad_vectors.reshape(own_blocks, BLOCK, emb_width)
    limit_rows = spend_limits.reshape(own_blocks, BLOCK)
    outbound = own_vectors[source].reshape(owner_total, capacity, BLOCK, emb_width)
    received = lax.all_to_all(outbound, "imp", split_axis=0, concat_axis=0, tiled=True)
    mine_vectors = received.reshape(slot_total, BLOCK, emb_width)[position]
    flat_vectors = mine_vectors.reshape(list_size * BLOCK, emb_width)
    value_matrix = jax.nn.softplus(
        lax.dot_general(
            imp_vectors, flat_vectors, (((1,), (1,)), ((), ())), preferred_element_type=jnp.float32
        )
    )

    def one_round(step, carry):
        pacing, prices = carry
        pace_out = pacing[source].reshape(owner_total, capacity, BLOCK)
        pace_in = lax.all_to_all(pace_out, "imp", split_axis=0, concat_axis=0, tiled=True).reshape(
            slot_total, BLOCK
        )
        pacing_columns = pace_in[position].reshape(-1)
        scaled_scores = value_matrix * pacing_columns[None, :] / softness_level
        run_top = jnp.max(scaled_scores, axis=1)
        run_sum = jnp.sum(jnp.exp(scaled_scores - run_top[:, None]), axis=1)
        row_top = lax.pmax(run_top, "ad")
        row_sum = lax.psum(run_sum * jnp.exp(run_top - row_top), "ad")
        log_sum_exponent = row_top + jnp.log(row_sum)
        new_prices = softness_level * log_sum_exponent
        share = jnp.exp(scaled_scores - log_sum_exponent[:, None])
        mine_util = jnp.sum(share * value_matrix, axis=0).reshape(list_size, BLOCK)
        spend_out = jnp.dot(placed_float, mine_util, precision=lax.Precision.HIGHEST)
        spend_in = lax.all_to_all(
            spend_out.reshape(owner_total, capacity, BLOCK),
            "imp",
            split_axis=0,
            concat_axis=0,
            tiled=True,
        ).reshape(slot_total, BLOCK)
        bidder_utility = jnp.dot(returned, spend_in, precision=lax.Precision.HIGHEST)
        target = jnp.minimum(limit_rows / jnp.maximum(bidder_utility, util_floor), pacing_cap)
        return (jnp.sqrt(pacing * target), new_prices)

    start = (
        jnp.ones((own_blocks, BLOCK), jnp.float32),
        jnp.zeros((imp_vectors.shape[0],), jnp.float32),
    )
    pacing, prices = lax.fori_loop(0, ROUNDS, one_round, start)
    return (pacing.reshape(-1), prices)


def solution(mesh):
    return jax.shard_map(
        per_device,
        mesh=mesh,
        in_specs=(P("imp", None), P(("imp", "ad"), None), P(("imp", "ad")), P("imp", "ad", None)),
        out_specs=(P(("imp", "ad")), P("imp")),
        check_vma=False,
    )
```

profile of v0, /device:TPU:1, one launch (start us, length us, event | category | flops | bytes accessed | tf_op | source)
XLA Modules:
  0.0 458.7 jit_solution(13744446227692678641)
XLA Ops:
  2.0 22.2 %all_to_all.29 = s32[64,1,2]{2,1,0:T(1,128)S(1)} all-to-all(s32[64,1,2]{2,1,0:T(1,128)S(1)} %bitcast.111), channel_id=1, replica_groups=mesh['imp'=64,'ad'=4] {'imp'}, dimensions={0} | all-to-all | bytes 1024 | tf_op jit(solution)/shard_map/all_to_all | solution.py:33
  34.7 95.7 %all-to-all-done.3 = bf16[64,2,128,128]{3,2,1,0:T(8,128)(2,1)} async-done(((bf16[64,2,128,128]{3,2,1,0:T(8,128)(2,1)}), bf16[64,2,128,128]{3,2,1,0:T(8,128)(2,1)}, u32[]{:S(2)}, u32[]{:S(2)}) %all-to-all-start.3) | async-done | bytes 4194336 | tf_op jit(solution)/shard_map/all_to_all | solution.py:44
  133.4 12.4 %compare_select_fusion.2 = f32[1024,4096]{0,1:T(8,128)} fusion(bf16[4096,128]{1,0:T(8,128)(2,1)S(1)} %bitcast.108, bf16[1024,128]{1,0:T(8,128)(2,1)S(1)} %copy-done.3), kind=kOutput, calls=%fused_computation.34 | convolution fusion | flops 1098907648 | bytes 18087936 | tf_op jit(solution)/shard_map/dot_general | solution.py:48
  145.8 17.5 %copy.11 = f32[1024,4096]{1,0:T(8,128)} copy(f32[1024,4096]{0,1:T(8,128)} %compare_select_fusion.2) | data formatting | bytes 33554432
  163.3 294.8 %while.15 = (s32[]{:T(128)}, f32[48,128]{1,0:T(8,128)S(1)}, f32[1024]{0:T(1024)}, s32[128]{0:T(128)S(1)}, s32[32]{0:T(128)S(1)}, /*index=5*/f32[1024,4096]{1,0:T...) while((s32[]{:T(128)}, f32[48,128]{1,0:T(8,128)S(1)}, ...), condition=%wide.region_9.10_spmd.clone.clone.clone, body=%wide.region_3.9_spmd.clone.clone.clone.sunk | while | flops 66114016 | bytes 51301680 | solution.py:85
  170.4 9.8 %all-to-all-done = f32[64,2,128]{2,1,0:T(2,128)S(1)} async-done(((f32[64,2,128]{2,1,0:T(2,128)}), f32[64,2,128]{2,1,0:T(2,128)S(1)}, u32[]{:S(2)}, u32[]{:S(2)}) %all-to-all-start) | async-done | bytes 65568 | tf_op jit(solution)/shard_map/while/body/eval_jaxpr/all_to_all | solution.py:56
  188.4 8.5 %pmax.11 = f32[1024]{0:T(1024)S(1)} all-reduce(f32[1024]{0:T(1024)S(1)} %fusion.44), channel_id=1, replica_groups=mesh['imp'=64,'ad'=4] {'ad'}, use_global_device_ids=true, to_apply=%region_5.5 | all-reduce | flops 1024 | bytes 8192 | tf_op jit(solution)/shard_map/while/body/eval_jaxpr/pmax | solution.py:63
  196.9 7.9 %exponential_reduce_fusion.2 = f32[1024]{0:T(1024)S(1)} fusion(f32[1024,4096]{1,0:T(8,128)} %get-tuple-element.257, f32[1024]{0:T(1024)S(1)} %fusion.44, f32[4096]{0:T(1024)S(1)} %bitcast.106), kind=kLoop, calls=%fused_computation.7.clone.1 | loop fusion | flops 16776192 | bytes 16801792 | tf_op jit(solution)/shard_map/while/body/eval_jaxpr/reduce_sum | solution.py:62
  211.4 8.0 %multiply_reduce_fusion.2 = f32[4096]{0:T(1024)S(1)} fusion(f32[1024,4096]{1,0:T(8,128)} %get-tuple-element.257, f32[1024]{0:T(1024)S(1)} %get-tuple-element.230, f32[4096]{0:T(1024)S(1)} %bitcast.107), kind=kLoop, calls=%fused_computation.6.clone.1 | loop fusion | flops 20967424 | bytes 16814080 | tf_op jit(solution)/shard_map/while/body/eval_jaxpr/reduce_sum | solution.py:68
  220.2 8.2 %all-to-all-start.1 = ((f32[64,2,128]{2,1,0:T(2,128)}), f32[64,2,128]{2,1,0:T(2,128)S(1)}, u32[]{:S(2)}, u32[]{:S(2)}) async-start(f32[64,2,128]{2,1,0:T(2,128)} %bitcast.99), calls=%async_computation.1 | async-start | bytes 131072 | tf_op jit(solution)/shard_map/while/body/eval_jaxpr/all_to_all | solution.py:70
  228.4 9.9 %all-to-all-done.1 = f32[64,2,128]{2,1,0:T(2,128)S(1)} async-done(((f32[64,2,128]{2,1,0:T(2,128)}), f32[64,2,128]{2,1,0:T(2,128)S(1)}, u32[]{:S(2)}, u32[]{:S(2)}) %all-to-all-start.1) | async-done | bytes 65568 | tf_op jit(solution)/shard_map/while/body/eval_jaxpr/all_to_all | solution.py:70
  244.2 9.9 %all-to-all-done = f32[64,2,128]{2,1,0:T(2,128)S(1)} async-done(((f32[64,2,128]{2,1,0:T(2,128)}), f32[64,2,128]{2,1,0:T(2,128)S(1)}, u32[]{:S(2)}, u32[]{:S(2)}) %all-to-all-start) | async-done | bytes 65568 | tf_op jit(solution)/shard_map/while/body/eval_jaxpr/all_to_all | solution.py:56
  284.6 8.0 %multiply_reduce_fusion.2 = f32[4096]{0:T(1024)S(1)} fusion(f32[1024,4096]{1,0:T(8,128)} %get-tuple-element.257, f32[1024]{0:T(1024)S(1)} %get-tuple-element.230, f32[4096]{0:T(1024)S(1)} %bitcast.107), kind=kLoop, calls=%fused_computation.6.clone.1 | loop fusion | flops 20967424 | bytes 16814080 | tf_op jit(solution)/shard_map/while/body/eval_jaxpr/reduce_sum | solution.py:68
  293.4 8.2 %all-to-all-start.1 = ((f32[64,2,128]{2,1,0:T(2,128)}), f32[64,2,128]{2,1,0:T(2,128)S(1)}, u32[]{:S(2)}, u32[]{:S(2)}) async-start(f32[64,2,128]{2,1,0:T(2,128)} %bitcast.99), calls=%async_computation.1 | async-start | bytes 131072 | tf_op jit(solution)/shard_map/while/body/eval_jaxpr/all_to_all | solution.py:70
  301.6 9.9 %all-to-all-done.1 = f32[64,2,128]{2,1,0:T(2,128)S(1)} async-done(((f32[64,2,128]{2,1,0:T(2,128)}), f32[64,2,128]{2,1,0:T(2,128)S(1)}, u32[]{:S(2)}, u32[]{:S(2)}) %all-to-all-start.1) | async-done | bytes 65568 | tf_op jit(solution)/shard_map/while/body/eval_jaxpr/all_to_all | solution.py:70
  317.4 9.9 %all-to-all-done = f32[64,2,128]{2,1,0:T(2,128)S(1)} async-done(((f32[64,2,128]{2,1,0:T(2,128)}), f32[64,2,128]{2,1,0:T(2,128)S(1)}, u32[]{:S(2)}, u32[]{:S(2)}) %all-to-all-start) | async-done | bytes 65568 | tf_op jit(solution)/shard_map/while/body/eval_jaxpr/all_to_all | solution.py:56
  357.8 8.0 %multiply_reduce_fusion.2 = f32[4096]{0:T(1024)S(1)} fusion(f32[1024,4096]{1,0:T(8,128)} %get-tuple-element.257, f32[1024]{0:T(1024)S(1)} %get-tuple-element.230, f32[4096]{0:T(1024)S(1)} %bitcast.107), kind=kLoop, calls=%fused_computation.6.clone.1 | loop fusion | flops 20967424 | bytes 16814080 | tf_op jit(solution)/shard_map/while/body/eval_jaxpr/reduce_sum | solution.py:68
  366.6 8.2 %all-to-all-start.1 = ((f32[64,2,128]{2,1,0:T(2,128)}), f32[64,2,128]{2,1,0:T(2,128)S(1)}, u32[]{:S(2)}, u32[]{:S(2)}) async-start(f32[64,2,128]{2,1,0:T(2,128)} %bitcast.99), calls=%async_computation.1 | async-start | bytes 131072 | tf_op jit(solution)/shard_map/while/body/eval_jaxpr/all_to_all | solution.py:70
  374.8 9.9 %all-to-all-done.1 = f32[64,2,128]{2,1,0:T(2,128)S(1)} async-done(((f32[64,2,128]{2,1,0:T(2,128)}), f32[64,2,128]{2,1,0:T(2,128)S(1)}, u32[]{:S(2)}, u32[]{:S(2)}) %all-to-all-start.1) | async-done | bytes 65568 | tf_op jit(solution)/shard_map/while/body/eval_jaxpr/all_to_all | solution.py:70
  390.6 9.9 %all-to-all-done = f32[64,2,128]{2,1,0:T(2,128)S(1)} async-done(((f32[64,2,128]{2,1,0:T(2,128)}), f32[64,2,128]{2,1,0:T(2,128)S(1)}, u32[]{:S(2)}, u32[]{:S(2)}) %all-to-all-start) | async-done | bytes 65568 | tf_op jit(solution)/shard_map/while/body/eval_jaxpr/all_to_all | solution.py:56
  416.4 7.9 %exponential_reduce_fusion.2 = f32[1024]{0:T(1024)S(1)} fusion(f32[1024,4096]{1,0:T(8,128)} %get-tuple-element.257, f32[1024]{0:T(1024)S(1)} %fusion.44, f32[4096]{0:T(1024)S(1)} %bitcast.106), kind=kLoop, calls=%fused_computation.7.clone.1 | loop fusion | flops 16776192 | bytes 16801792 | tf_op jit(solution)/shard_map/while/body/eval_jaxpr/reduce_sum | solution.py:62
  430.9 8.0 %multiply_reduce_fusion.2 = f32[4096]{0:T(1024)S(1)} fusion(f32[1024,4096]{1,0:T(8,128)} %get-tuple-element.257, f32[1024]{0:T(1024)S(1)} %get-tuple-element.230, f32[4096]{0:T(1024)S(1)} %bitcast.107), kind=kLoop, calls=%fused_computation.6.clone.1 | loop fusion | flops 20967424 | bytes 16814080 | tf_op jit(solution)/shard_map/while/body/eval_jaxpr/reduce_sum | solution.py:68
  439.8 8.2 %all-to-all-start.1 = ((f32[64,2,128]{2,1,0:T(2,128)}), f32[64,2,128]{2,1,0:T(2,128)S(1)}, u32[]{:S(2)}, u32[]{:S(2)}) async-start(f32[64,2,128]{2,1,0:T(2,128)} %bitcast.99), calls=%async_computation.1 | async-start | bytes 131072 | tf_op jit(solution)/shard_map/while/body/eval_jaxpr/all_to_all | solution.py:70
  448.0 9.9 %all-to-all-done.1 = f32[64,2,128]{2,1,0:T(2,128)S(1)} async-done(((f32[64,2,128]{2,1,0:T(2,128)}), f32[64,2,128]{2,1,0:T(2,128)S(1)}, u32[]{:S(2)}, u32[]{:S(2)}) %all-to-all-start.1) | async-done | bytes 65568 | tf_op jit(solution)/shard_map/while/body/eval_jaxpr/all_to_all | solution.py:70
  (91 shorter events, 141.7 us)
Async XLA Ops:
  0.6 25.1 %copy-start = (bf16[6144,128]{1,0:T(8,128)(2,1)S(1)}, bf16[6144,128]{1,0:T(8,128)(2,1)}, u32[]{:S(2)}) copy-start(bf16[6144,128]{1,0:T(8,128)(2,1)} %param.7) | copy-start | bytes 4718596
  0.6 33.9 %copy-start.4 = (s32[1,1,32]{2,1,0:T(1,128)S(1)}, s32[1,1,32]{2,1,0:T(1,128)}, u32[]{:S(2)}) copy-start(s32[1,1,32]{2,1,0:T(1,128)} %param.9) | copy-start | bytes 388
  0.7 132.7 %copy-start.3 = (bf16[1024,128]{1,0:T(8,128)(2,1)S(1)}, bf16[1024,128]{1,0:T(8,128)(2,1)}, u32[]{:S(2)}) copy-start(bf16[1024,128]{1,0:T(8,128)(2,1)} %param.6) | copy-start | bytes 786436
  28.8 101.6 %all-to-all-start.3 = ((bf16[64,2,128,128]{3,2,1,0:T(8,128)(2,1)}), bf16[64,2,128,128]{3,2,1,0:T(8,128)(2,1)}, u32[]{:S(2)}, u32[]{:S(2)}) async-start(bf16[64,2,128,128]{3,2,1,0:T(8,128)(2,1)} %bitcast.102), calls=%async_computation.3 | async-start | bytes 8388608 | tf_op jit(solution)/shard_map/all_to_all | solution.py:44
  145.8 17.5 %copy-start.2 = (f32[6144]{0:T(1024)S(1)}, f32[6144]{0:T(1024)}, u32[]{:S(2)}) copy-start(f32[6144]{0:T(1024)} %param.8) | copy-start | bytes 73732
  164.6 15.6 %all-to-all-start = ((f32[64,2,128]{2,1,0:T(2,128)}), f32[64,2,128]{2,1,0:T(2,128)S(1)}, u32[]{:S(2)}, u32[]{:S(2)}) async-start(f32[64,2,128]{2,1,0:T(2,128)} %bitcast.96), calls=%async_computation | async-start | bytes 131072 | tf_op jit(solution)/shard_map/while/body/eval_jaxpr/all_to_all | solution.py:56
  220.2 18.1 %all-to-all-start.1 = ((f32[64,2,128]{2,1,0:T(2,128)}), f32[64,2,128]{2,1,0:T(2,128)S(1)}, u32[]{:S(2)}, u32[]{:S(2)}) async-start(f32[64,2,128]{2,1,0:T(2,128)} %bitcast.99), calls=%async_computation.1 | async-start | bytes 131072 | tf_op jit(solution)/shard_map/while/body/eval_jaxpr/all_to_all | solution.py:70
  239.8 14.3 %all-to-all-start = ((f32[64,2,128]{2,1,0:T(2,128)}), f32[64,2,128]{2,1,0:T(2,128)S(1)}, u32[]{:S(2)}, u32[]{:S(2)}) async-start(f32[64,2,128]{2,1,0:T(2,128)} %bitcast.96), calls=%async_computation | async-start | bytes 131072 | tf_op jit(solution)/shard_map/while/body/eval_jaxpr/all_to_all | solution.py:56
  293.4 18.1 %all-to-all-start.1 = ((f32[64,2,128]{2,1,0:T(2,128)}), f32[64,2,128]{2,1,0:T(2,128)S(1)}, u32[]{:S(2)}, u32[]{:S(2)}) async-start(f32[64,2,128]{2,1,0:T(2,128)} %bitcast.99), calls=%async_computation.1 | async-start | bytes 131072 | tf_op jit(solution)/shard_map/while/body/eval_jaxpr/all_to_all | solution.py:70
  313.0 14.3 %all-to-all-start = ((f32[64,2,128]{2,1,0:T(2,128)}), f32[64,2,128]{2,1,0:T(2,128)S(1)}, u32[]{:S(2)}, u32[]{:S(2)}) async-start(f32[64,2,128]{2,1,0:T(2,128)} %bitcast.96), calls=%async_computation | async-start | bytes 131072 | tf_op jit(solution)/shard_map/while/body/eval_jaxpr/all_to_all | solution.py:56
  366.6 18.1 %all-to-all-start.1 = ((f32[64,2,128]{2,1,0:T(2,128)}), f32[64,2,128]{2,1,0:T(2,128)S(1)}, u32[]{:S(2)}, u32[]{:S(2)}) async-start(f32[64,2,128]{2,1,0:T(2,128)} %bitcast.99), calls=%async_computation.1 | async-start | bytes 131072 | tf_op jit(solution)/shard_map/while/body/eval_jaxpr/all_to_all | solution.py:70
  386.1 14.3 %all-to-all-start = ((f32[64,2,128]{2,1,0:T(2,128)}), f32[64,2,128]{2,1,0:T(2,128)S(1)}, u32[]{:S(2)}, u32[]{:S(2)}) async-start(f32[64,2,128]{2,1,0:T(2,128)} %bitcast.96), calls=%async_computation | async-start | bytes 131072 | tf_op jit(solution)/shard_map/while/body/eval_jaxpr/all_to_all | solution.py:56
  439.8 18.1 %all-to-all-start.1 = ((f32[64,2,128]{2,1,0:T(2,128)}), f32[64,2,128]{2,1,0:T(2,128)S(1)}, u32[]{:S(2)}, u32[]{:S(2)}) async-start(f32[64,2,128]{2,1,0:T(2,128)} %bitcast.99), calls=%async_computation.1 | async-start | bytes 131072 | tf_op jit(solution)/shard_map/while/body/eval_jaxpr/all_to_all | solution.py:70
  458.1 0.6 copy-start.1
where the time goes:
time: 460 us; the launch traced here: 459 us
  waiting for transfers between devices  175 us (38%)
  other arithmetic  98.7 us (21%)
  blocking collectives  78 us (17%)
  starting transfers between devices  57.5 us (12%)
  local copies, waits for them, and re-layouts  32.2 us (7%)
  matrix products  16.5 us (4%)
    all_to_all x1, waiting for transfers between devices, per_device(): lax.all_to_all(outbound, 'imp', split_axis=0, concat_axis=0, tiled=True)  95.7 us
    all_to_all x4, waiting for transfers between devices, one_round(): lax.all_to_all(spend_out.reshape(owner_total, capacity, BLOCK), 'imp', sp...  39.6 us
    all_to_all x4, waiting for transfers between devices, one_round(): lax.all_to_all(pace_out, 'imp', split_axis=0, concat_axis=0, tiled=True)  39.4 us
    all_to_all x4, starting transfers between devices, one_round(): lax.all_to_all(spend_out.reshape(owner_total, capacity, BLOCK), 'imp', sp...  32.7 us
    reduce_sum x4, other arithmetic, one_round(): mine_util = jnp.sum(share * value_matrix, axis=0).reshape(list_size, BLOCK)  32.1 us
    pmax x4, blocking collectives, one_round(): row_top = lax.pmax(run_top, 'ad')  31.7 us
    reduce_sum x4, other arithmetic, one_round(): run_sum = jnp.sum(jnp.exp(scaled_scores - run_top[:, None]), axis=1)  31.5 us
    reduce_max x4, other arithmetic, one_round(): run_top = jnp.max(scaled_scores, axis=1)  30.6 us
  transfers between devices with their start and end apart: 9, of which 9 were waited for; matrix products, arithmetic and copies ran while one was open for 0% of the time, Pallas kernels for 0%

commit v1 on v0

v1 whole, which is shorter than its diff:
```python
import functools
import math

import jax
import jax.numpy as jnp
from jax import lax
from jax.experimental import pallas as pl
from jax.experimental.pallas import tpu as pltpu
from jax.sharding import PartitionSpec as P

BLOCK = 128
ROUNDS = 4
CAP = 2
SHARED = 6
SLOTS = SHARED + CAP

softness_level = 0.5
util_floor = 0.01
pacing_cap = 3.0

LOG2E = math.log2(math.e)
LN2 = math.log(2.0)
SCALE = LOG2E / softness_level
HI = lax.Precision.HIGHEST
f32 = jnp.float32
bf16 = jnp.bfloat16
VMEM = pl.BlockSpec(memory_space=pltpu.VMEM)


def params(mib):
    return pltpu.CompilerParams(vmem_limit_bytes=mib * 2**20)


def pinned(x):
    return pltpu.with_memory_space_constraint(x, pltpu.VMEM)


def tn(a, b):
    return lax.dot_general(a, b, (((0,), (0,)), ((), ())), precision=HI, preferred_element_type=f32)


def nn(a, b):
    return lax.dot_general(a, b, (((1,), (0,)), ((), ())), precision=HI, preferred_element_type=f32)


def eye():
    return lax.broadcasted_iota(jnp.int32, (128, 128), 0) == lax.broadcasted_iota(
        jnp.int32, (128, 128), 1
    )


def values_kernel(blocks, x_ref, y_ref, v_ref, ya, yb, yt):
    parts = y_ref.shape[0] // blocks
    ya[...] = y_ref[:, :128].astype(f32)
    yb[...] = y_ref[:, 128:].astype(f32)

    def unpack(k, _):
        at = pl.multiple_of(k * BLOCK, BLOCK)
        yt[pl.ds(at, parts), :] = ya[pl.ds(k, parts, stride=blocks), :].astype(bf16)
        yt[pl.ds(at + parts, parts), :] = yb[pl.ds(k, parts, stride=blocks), :].astype(bf16)
        return 0

    lax.fori_loop(0, blocks, unpack, 0)
    tile_r, tile_c = 256, 512
    across = v_ref.shape[1] // tile_c

    def tile(step, _):
        rows = pl.ds(pl.multiple_of((step // across) * tile_r, tile_r), tile_r)
        cols = pl.ds(pl.multiple_of((step % across) * tile_c, tile_c), tile_c)
        s = lax.dot_general(
            x_ref[rows, :], yt[cols, :], (((1,), (1,)), ((), ())), preferred_element_type=f32
        )
        v_ref[rows, cols] = jnp.maximum(s, 0.0) + LN2 * jnp.log2(1.0 + jnp.exp2(jnp.abs(s) * -LOG2E))
        return 0

    lax.fori_loop(0, (v_ref.shape[0] // tile_r) * across, tile, 0)


def values_call(x, y, blocks):
    rows, width = x.shape[0], blocks * BLOCK
    return pl.pallas_call(
        functools.partial(values_kernel, blocks),
        out_shape=pltpu.VMEM((rows, width), f32),
        in_specs=[VMEM, VMEM],
        out_specs=VMEM,
        scratch_shapes=[
            pltpu.VMEM((y.shape[0], 128), f32),
            pltpu.VMEM((y.shape[0], 128), f32),
            pltpu.VMEM((width, 128), bf16),
        ],
        compiler_params=params(16),
    )(x, y)


def score(v_ref, ev_ref, ms_ref, pace, mcol, scol):
    rows, width = v_ref.shape
    step_rows = 32

    def body(step, _):
        for part in range(step_rows // 8):
            at = pl.ds(pl.multiple_of(step * step_rows, step_rows) + part * 8, 8)
            v = v_ref[at, :]
            t = v * pace[...]
            m = jnp.max(t, axis=1, keepdims=True)
            e = jnp.exp2(t - m)
            ev_ref[at, :] = e * v
            mcol[at, :] = jnp.broadcast_to(m, (8, 128))
            scol[at, :] = jnp.broadcast_to(jnp.sum(e, axis=1, keepdims=True), (8, 128))
        return 0

    lax.fori_loop(0, rows // step_rows, body, 0)
    diagonal = eye()
    chunks = rows // 128
    for c in range(chunks):
        part = pl.ds(c * 128, 128)
        ms_ref[c : c + 1, :] = jnp.sum(jnp.where(diagonal, mcol[part, :], 0.0), axis=0, keepdims=True)
        ms_ref[chunks + c : chunks + c + 1, :] = jnp.sum(
            jnp.where(diagonal, scol[part, :], 0.0), axis=0, keepdims=True
        )


def first_score_kernel(flag_ref, v_ref, ev_ref, ms_ref, pace, mcol, scol):
    pace[...] = jnp.full(pace.shape, SCALE, f32)
    ms_ref[16:24, :] = flag_ref[...]
    score(v_ref, ev_ref, ms_ref, pace, mcol, scol)


def pace_step(pace, util, limit):
    return jnp.sqrt(pace * jnp.minimum(limit / jnp.maximum(util, util_floor), pacing_cap))


def spread_pace(p, pace):
    for k in range(p.shape[0]):
        pace[:, k * BLOCK : (k + 1) * BLOCK] = jnp.broadcast_to(p[k : k + 1, :] * SCALE, (8, BLOCK))


def second_score_kernel(
    util_ref, recv_ref, pick_ref, extra_ref, v_ref, ev_ref, ms_ref, p_ref, limit_ref, pace, mcol, scol
):
    blocks = util_ref.shape[0]
    got = tn(pick_ref[...], recv_ref[...])
    util = util_ref[...] + extra_ref[...] + got[:blocks, :]
    limit = got[blocks:, :]
    p = pace_step(jnp.ones(util.shape, f32), util, limit)
    p_ref[...] = p
    limit_ref[...] = limit
    spread_pace(p, pace)
    score(v_ref, ev_ref, ms_ref, pace, mcol, scol)


def score_kernel(
    util_ref, recv_ref, pick_ref, extra_ref, limit_ref, old_ref, v_ref, ev_ref, ms_ref, p_ref, pace, mcol, scol
):
    util = util_ref[...] + extra_ref[...] + tn(pick_ref[...], recv_ref[...])
    p = pace_step(old_ref[...], util, limit_ref[...])
    p_ref[...] = p
    spread_pace(p, pace)
    score(v_ref, ev_ref, ms_ref, pace, mcol, scol)


def score_call(kernel, v, args, ms_rows, outs):
    rows, width = v.shape
    small = jax.ShapeDtypeStruct((width // BLOCK, BLOCK), f32)
    return pl.pallas_call(
        kernel,
        out_shape=[pltpu.VMEM((rows, width), f32), jax.ShapeDtypeStruct((ms_rows, 128), f32)] + [small] * outs,
        in_specs=[VMEM] * (len(args) + 1),
        out_specs=[VMEM] * (2 + outs),
        scratch_shapes=[
            pltpu.VMEM((8, width), f32),
            pltpu.VMEM((rows, 128), f32),
            pltpu.VMEM((rows, 128), f32),
        ],
        compiler_params=params(16),
    )(*args, pinned(v))


def combine(ms_ref, all_ref, chunks):
    tops = all_ref[:, 0:chunks, :]
    sums = all_ref[:, chunks : 2 * chunks, :]
    top = jnp.max(tops, axis=0)
    total = jnp.sum(sums * jnp.exp2(tops - top[None]), axis=0)
    lse = top + jnp.log2(total)
    return lse, jnp.exp2(ms_ref[0:chunks, :] - lse)


def utility(weight, ev_ref, util_ref, wcol):
    rows, width = ev_ref.shape
    diagonal = eye()
    for c in range(rows // 128):
        spread = jnp.where(diagonal, jnp.broadcast_to(weight[c : c + 1, :], (128, 128)), 0.0)
        wcol[c * 128 : (c + 1) * 128, :] = jnp.broadcast_to(
            jnp.sum(spread, axis=1, keepdims=True), (128, 128)
        )
    blocks = width // BLOCK

    def body(step, acc):
        out = list(acc)
        for part in range(2):
            at = pl.ds(pl.multiple_of(step * 16, 16) + part * 8, 8)
            w = wcol[at, :]
            for k in range(blocks):
                out[k] = out[k] + ev_ref[at, k * BLOCK : (k + 1) * BLOCK] * w
        return tuple(out)

    acc = lax.fori_loop(0, rows // 16, body, tuple(jnp.zeros((8, BLOCK), f32) for _ in range(blocks)))
    for k in range(blocks):
        util_ref[k : k + 1, :] = jnp.sum(acc[k], axis=0, keepdims=True)


def first_utility_kernel(ms_ref, all_ref, put_ref, own_put_ref, limit_ref, ev_ref, util_ref, send_ref, wcol):
    _, weight = combine(ms_ref, all_ref, ev_ref.shape[0] // 128)
    utility(weight, ev_ref, util_ref, wcol)
    send_ref[...] = nn(put_ref[...], util_ref[...]) + nn(own_put_ref[...], limit_ref[...])


def utility_kernel(ms_ref, all_ref, put_ref, ev_ref, util_ref, send_ref, wcol):
    _, weight = combine(ms_ref, all_ref, ev_ref.shape[0] // 128)
    utility(weight, ev_ref, util_ref, wcol)
    send_ref[...] = nn(put_ref[...], util_ref[...])


def last_utility_kernel(ms_ref, all_ref, put_ref, p_ref, ev_ref, util_ref, send_ref, price_ref, wcol):
    lse, weight = combine(ms_ref, all_ref, ev_ref.shape[0] // 128)
    price_ref[...] = lse * (softness_level * LN2)
    utility(weight, ev_ref, util_ref, wcol)
    send_ref[:, :BLOCK] = nn(put_ref[...], util_ref[...])
    send_ref[:, BLOCK:] = nn(put_ref[...], p_ref[...])


def utility_call(kernel, ev, args, send_shape, price):
    rows, width = ev.shape
    outs = [
        jax.ShapeDtypeStruct((width // BLOCK, BLOCK), f32),
        jax.ShapeDtypeStruct(send_shape, f32),
    ]
    if price:
        outs.append(jax.ShapeDtypeStruct((rows // 128, 128), f32))
    return pl.pallas_call(
        kernel,
        out_shape=outs,
        in_specs=[VMEM] * (len(args) + 1),
        out_specs=[VMEM] * len(outs),
        scratch_shapes=[pltpu.VMEM((rows, 128), f32)],
        compiler_params=params(16),
    )(*args, pinned(ev))


def last_pace_kernel(recv_ref, back_ref, limit_ref, out_ref):
    back = back_ref[...]
    limit = limit_ref[...]
    got = nn(back, recv_ref[...])
    count = jnp.sum(back, axis=1, keepdims=True)
    lone = jnp.ones(limit.shape, f32)
    for _ in range(ROUNDS - 1):
        lone = pace_step(lone, jnp.zeros(limit.shape, f32), limit)
    pace = jnp.where(count > 0.0, got[:, BLOCK:] / jnp.maximum(count, 1.0), lone)
    out_ref[...] = pace_step(pace, got[:, :BLOCK], limit)


def before(flags, axis):
    size = flags.shape[axis]
    order = jnp.arange(size)
    less = (order[:, None] < order[None, :]).astype(f32)
    moved = jnp.moveaxis(flags, axis, -1).astype(f32)
    return jnp.moveaxis(jnp.dot(moved, less), -1, axis).astype(jnp.int32)


def swap(x, axis):
    return lax.all_to_all(x, axis, split_axis=0, concat_axis=0, tiled=True)


def per_device(imp_vectors, ad_vectors, spend_limits, targets):
    owners = lax.axis_size("imp")
    columns = lax.axis_size("ad")
    me = lax.axis_index("imp")
    emb = imp_vectors.shape[1]
    own_blocks = ad_vectors.shape[0] // BLOCK
    wanted = targets.reshape(-1)
    size = wanted.shape[0]
    half = BLOCK // 2
    limits = spend_limits.reshape(own_blocks, BLOCK)

    lists = swap(jnp.broadcast_to(wanted[None, :], (owners, size)), "imp")
    pieces = ad_vectors.reshape(own_blocks, 2, half, emb).transpose(2, 0, 1, 3)
    table = swap(pieces.reshape(half, own_blocks, 2 * emb), "imp").reshape(owners * own_blocks, 2 * emb)
    chosen = table[lists.reshape(-1)].reshape(owners, size, 2 * emb)
    mine = swap(chosen, "imp").reshape(owners * size, 2 * emb)

    peer = jnp.arange(owners, dtype=jnp.int32)
    equal = (lists[:, :, None] == wanted[None, None, :]) & (peer != me)[:, None, None]
    gives = jnp.any(equal, axis=1)
    takes = jnp.any(equal, axis=2)
    slot = jnp.arange(SLOTS, dtype=jnp.int32)
    give_at = before(gives, 1)
    take_at = before(takes, 1)
    usable = (slot < SHARED)[None, :, None]
    put = ((give_at[:, None, :] == slot[None, :, None]) & gives[:, None, :] & usable).astype(f32)
    take_slot = ((take_at[:, None, :] == slot[None, :, None]) & takes[:, None, :] & usable).astype(f32)
    pick = jnp.einsum("isk,ikw->isw", take_slot, equal.astype(f32))
    put = put.reshape(owners * SLOTS, size)
    pick = pick.reshape(owners * SLOTS, size)
    holds = jnp.any(
        lists[:, :, None] == jnp.arange(owners * own_blocks, dtype=jnp.int32)[None, None, :], axis=1
    ).astype(bf16)
    common = lax.dot_general(holds, holds, (((1,), (1,)), ((), ())), preferred_element_type=f32)
    crowded = jnp.any((common > SHARED + 0.5) & (peer[:, None] != peer[None, :]))

    owner_of = wanted // own_blocks
    rank_of = jnp.sum(
        (owner_of[:, None] == owner_of[None, :]) & (jnp.arange(size)[None, :] < jnp.arange(size)[:, None]),
        axis=1,
    )
    lane = jnp.arange(CAP, dtype=jnp.int32)
    placed = (
        (owner_of[None, None, :] == peer[:, None, None]) & (rank_of[None, None, :] == lane[None, :, None])
    ).astype(f32)
    at_me = lists // own_blocks == me
    asked_at = before(at_me, 1)
    asked = (asked_at[:, None, :] == lane[None, :, None]) & at_me[:, None, :]
    local = jnp.arange(own_blocks, dtype=jnp.int32)
    here = (lists[:, :, None] - me * own_blocks) == local[None, None, :]
    back = jnp.einsum("irk,ikl->irl", asked.astype(f32), here.astype(f32))
    own_put = jnp.concatenate([jnp.zeros((owners, SHARED, own_blocks), f32), back], axis=1)
    own_put = own_put.reshape(owners * SLOTS, own_blocks)
    limit_pick = jnp.concatenate([jnp.zeros((owners, SHARED, size), f32), placed], axis=1)
    limit_pick = limit_pick.reshape(owners * SLOTS, size)
    placed = placed.reshape(owners * CAP, size)
    back = back.reshape(owners * CAP, own_blocks).T

    values = values_call(imp_vectors, mine, size)
    wide_pick = equal.astype(f32).reshape(owners * size, size)

    def wide(util):
        everyone = swap(jnp.broadcast_to(util[None], (owners, size, BLOCK)), "imp")
        return jnp.einsum("jk,jb->kb", wide_pick, everyone.reshape(owners * size, BLOCK), precision=HI)

    def combine_columns(ms):
        return swap(jnp.broadcast_to(ms[None], (columns,) + ms.shape), "ad")

    def exchange(send):
        return swap(send.reshape(owners, SLOTS, BLOCK), "imp").reshape(owners * SLOTS, BLOCK)

    flag = jnp.broadcast_to(crowded.astype(f32), (8, 128))
    ev, ms = score_call(first_score_kernel, values, [flag], 24, 0)
    every = combine_columns(ms)
    over = jnp.max(every[:, 16, 0]) > 0.5
    pick = jnp.where(over, 0.0, pick)
    util, send = utility_call(
        first_utility_kernel, ev, [ms, every, put, own_put, limits], (owners * SLOTS, BLOCK), False
    )
    recv = exchange(send)
    extra = lax.cond(over, wide, jnp.zeros_like, util)
    ev, ms, pace, wanted_limits = score_call(
        second_score_kernel, values, [util, recv, jnp.concatenate([pick, limit_pick], axis=1), extra], 16, 2
    )
    for step in range(2, ROUNDS):
        every = combine_columns(ms)
        util, send = utility_call(utility_kernel, ev, [ms, every, put], (owners * SLOTS, BLOCK), False)
        recv = exchange(send)
        extra = lax.cond(over, wide, jnp.zeros_like, util)
        ev, ms, pace = score_call(score_kernel, values, [util, recv, pick, extra, wanted_limits, pace], 16, 1)
    every = combine_columns(ms)
    util, send, prices = utility_call(
        last_utility_kernel, ev, [ms, every, placed, pace], (owners * CAP, 2 * BLOCK), True
    )
    recv = swap(send.reshape(owners, CAP, 2 * BLOCK), "imp").reshape(owners * CAP, 2 * BLOCK)
    final = pl.pallas_call(
        last_pace_kernel,
        out_shape=jax.ShapeDtypeStruct((own_blocks, BLOCK), f32),
        in_specs=[VMEM] * 3,
        out_specs=VMEM,
    )(recv, back, limits)
    return final.reshape(-1), prices.reshape(-1)


def solution(mesh):
    return jax.shard_map(
        per_device,
        mesh=mesh,
        in_specs=(P("imp", None), P(("imp", "ad"), None), P(("imp", "ad")), P("imp", "ad", None)),
        out_specs=(P(("imp", "ad")), P("imp")),
        check_vma=False,
    )
```

time: 460 us -> 355 us (0.77); the launches traced: 459 us -> 349 us
  waiting for transfers between devices: 175 us -> 84.8 us
  other arithmetic: 98.7 us -> 17.5 us
  Pallas kernels: 0 us -> 60.7 us
  local copies, waits for them, and re-layouts: 32.2 us -> 84.4 us
  blocking collectives: 78 us -> 44.6 us
  matrix products: 16.5 us -> 2.67 us
  starting transfers between devices: 57.5 us -> 51.4 us
    all_to_all x9 -> x8, waiting for transfers between devices: 175 us -> 84.8 us  [swap(): return lax.all_to_all(x, axis, split_axis=0, concat_axis=0, tiled=True)]
    reduce_sum x10 -> x1, other arithmetic: 63.8 us -> 0.18 us  [per_device(): jnp.sum((owner_of[:, None] == owner_of[None, :]) & (jnp.arange(size)[None...]
    pallas_call x0 -> x10, Pallas kernels: none -> 60.7 us  [the longest x4 35.8 us: score_call(): pl.pallas_call(kernel, out_shape=[pltpu.VMEM((rows, width), f32), jax.Sha...]
    unnamed x11 -> x28, local copies, waits for them, and re-layouts: 18.1 us -> 63.3 us
    pmax x4 -> x0, blocking collectives: 31.7 us -> none  [one_round(): row_top = lax.pmax(run_top, 'ad')]
    reduce_max x4 -> x1, other arithmetic: 30.6 us -> 0.6 us  [per_device(): over = jnp.max(every[:, 16, 0]) > 0.5]
    psum x4 -> x0, blocking collectives: 24.1 us -> none  [one_round(): row_sum = lax.psum(run_sum * jnp.exp(run_top - row_top), 'ad')]
    all_to_all x1 -> x3, blocking collectives: 22.2 us -> 44.6 us  [swap(): return lax.all_to_all(x, axis, split_axis=0, concat_axis=0, tiled=True)]
  transfers between devices with their start and end apart: 9 -> 8, of which waited for: 9 -> 8; matrix products, arithmetic and copies ran while one was open for 0% -> 8% of each run, Pallas kernels for 0% -> 0%
where the time goes in v1:
time: 355 us; the launch traced here: 349 us
  waiting for transfers between devices  84.8 us (24%)
  local copies, waits for them, and re-layouts  84.4 us (24%)
  Pallas kernels  60.7 us (17%)
  starting transfers between devices  51.4 us (14%)
  blocking collectives  44.6 us (13%)
  other arithmetic  17.5 us (5%)
    all_to_all x8, waiting for transfers between devices, swap(): return lax.all_to_all(x, axis, split_axis=0, concat_axis=0, tiled=True)  84.8 us
    unnamed x28, local copies, waits for them, and re-layouts  63.3 us
    all_to_all x8, starting transfers between devices, swap(): return lax.all_to_all(x, axis, split_axis=0, concat_axis=0, tiled=True)  51.4 us
    all_to_all x3, blocking collectives, swap(): return lax.all_to_all(x, axis, split_axis=0, concat_axis=0, tiled=True)  44.6 us
    pallas_call x4, Pallas kernels, score_call(): pl.pallas_call(kernel, out_shape=[pltpu.VMEM((rows, width), f32), jax.Sha...  35.8 us
    pallas_call x1, Pallas kernels, values_call(): pl.pallas_call(functools.partial(values_kernel, blocks), out_shape=pltpu....  12.4 us
    reduce_or x1, other arithmetic, per_device(): jnp.any(lists[:, :, None] == jnp.arange(owners * own_blocks, dtype=jnp.in...  11 us
    pallas_call x4, Pallas kernels, utility_call(): pl.pallas_call(kernel, out_shape=outs, in_specs=[VMEM] * (len(args) + 1),...  10.7 us
  transfers between devices with their start and end apart: 8, of which 8 were waited for; matrix products, arithmetic and copies ran while one was open for 8% of the time, Pallas kernels for 0%

profile of v1, /device:TPU:1, one launch (start us, length us, event | category | flops | bytes accessed | tf_op | source)
XLA Modules:
  0.0 348.9 jit_solution(6750914104773680730)
XLA Ops:
  2.0 13.2 %all-to-all-start.3 = ((s32[64,1,32]{2,1,0:T(1,128)}), s32[64,1,32]{2,1,0:T(1,128)S(1)}, u32[]{:S(2)}, u32[]{:S(2)}) async-start(s32[64,1,32]{2,1,0:T(1,128)} %broadcast_in_dim.21), calls=%async_computation.3 | async-start | bytes 65536 | tf_op jit(solution)/shard_map/all_to_all | solution.py:270
  24.4 6.4 %all-to-all-start.4 = ((bf16[64,48,256]{2,1,0:T(8,128)(2,1)}), bf16[64,48,256]{2,1,0:T(8,128)(2,1)S(1)}, u32[]{:S(2)}, u32[]{:S(2)}) async-start(bf16[64,48,256]{2,1,0:T(8,128)(2,1)} %reshape.242), calls=%async_computation.4 | async-start | bytes 3145728 | tf_op jit(solution)/shard_map/all_to_all | solution.py:270
  36.9 33.7 %all-to-all-done.4 = bf16[64,48,256]{2,1,0:T(8,128)(2,1)S(1)} async-done(((bf16[64,48,256]{2,1,0:T(8,128)(2,1)}), bf16[64,48,256]{2,1,0:T(8,128)(2,1)S(1)}, u32[]{:S(2)}, u32[]{:S(2)}) %all-to-all-start.4) | async-done | bytes 1572896 | tf_op jit(solution)/shard_map/all_to_all | solution.py:270
  70.6 9.0 %gather_fusion = bf16[2048,256]{1,0:T(8,128)(2,1)} fusion(bf16[3072,256]{1,0:T(8,128)(2,1)S(1)} %bitcast.65, s32[2048]{0:T(1024)S(1)} %broadcast_clamp_fusion), kind=kCustom, calls=%fused_computation | custom fusion | bytes 2105344 | tf_op jit(solution)/shard_map/gather | solution.py:287
  79.6 6.3 %all-to-all-start.5 = ((bf16[64,32,256]{2,1,0:T(8,128)(2,1)}), bf16[64,32,256]{2,1,0:T(8,128)(2,1)S(1)}, u32[]{:S(2)}, u32[]{:S(2)}) async-start(bf16[64,32,256]{2,1,0:T(8,128)(2,1)} %bitcast.9), calls=%async_computation.5 | async-start | bytes 2097152 | tf_op jit(solution)/shard_map/all_to_all | solution.py:270
  86.5 11.0 %fusion = pred[64,3072]{1,0:T(8,128)(4,1)S(1)} fusion(s32[64,32]{1,0:T(8,128)S(1)} %bitcast.72), kind=kLoop, calls=%fused_computation.2 | loop fusion | flops 12386304 | bytes 204800 | tf_op jit(solution)/shard_map/reduce_or | solution.py:303
  100.6 13.7 %all-to-all-done.5 = bf16[64,32,256]{2,1,0:T(8,128)(2,1)S(1)} async-done(((bf16[64,32,256]{2,1,0:T(8,128)(2,1)}), bf16[64,32,256]{2,1,0:T(8,128)(2,1)S(1)}, u32[]{:S(2)}, u32[]{:S(2)}) %all-to-all-start.5) | async-done | bytes 1048608 | tf_op jit(solution)/shard_map/all_to_all | solution.py:270
  114.2 12.4 %shard_map.62.v_ref = f32[1024,4096]{1,0:T(8,128)S(1)} custom-call(bf16[1024,128]{1,0:T(8,128)(2,1)S(1)} %copy-done.11, bf16[2048,256]{1,0:T(8,128)(2,1)S(1)} %bitcast.56), custom_call_target="tpu_custom_call" | custom-call | tf_op jit(solution)/shard_map/pallas_call | solution.py:81
  138.2 8.7 %shard_map.63 = (f32[1024,4096]{1,0:T(8,128)S(1)}, f32[24,128]{1,0:T(8,128)S(1)}) custom-call(f32[8,128]{1,0:T(8,128)S(1)} %broadcast_in_dim.22.flag_ref, f32[1024,4096]{1,0:T(8,128)S(1)} %copy-done.1), custom_call_target="tpu_custom_call" | custom-call | tf_op jit(solution)/shard_map/pallas_call | solution.py:164
  172.2 7.5 %all-to-all-start.7 = ((f32[64,8,128]{2,1,0:T(8,128)}), f32[64,8,128]{2,1,0:T(8,128)S(1)}, u32[]{:S(2)}, u32[]{:S(2)}) async-start(f32[64,8,128]{2,1,0:T(8,128)} %bitcast.16), calls=%async_computation.7 | async-start | bytes 524288 | tf_op jit(solution)/shard_map/all_to_all | solution.py:270
  180.7 11.0 %all-to-all-done.7 = f32[64,8,128]{2,1,0:T(8,128)S(1)} async-done(((f32[64,8,128]{2,1,0:T(8,128)}), f32[64,8,128]{2,1,0:T(8,128)S(1)}, u32[]{:S(2)}, u32[]{:S(2)}) %all-to-all-start.7) | async-done | bytes 262176 | tf_op jit(solution)/shard_map/all_to_all | solution.py:270
  191.7 5.8 %copy-done.2 = f32[1024,4096]{1,0:T(8,128)S(1)} copy-done((f32[1024,4096]{1,0:T(8,128)S(1)}, f32[1024,4096]{1,0:T(8,128)}, u32[]{:S(2)}) %copy-start.2) | copy-done | bytes 16777240
  197.4 9.1 %shard_map.65 = (f32[1024,4096]{1,0:T(8,128)S(1)}, f32[16,128]{1,0:T(8,128)S(1)}, f32[32,128]{1,0:T(8,128)S(1)}, f32[32,128]{1,0:T(8,128)S(1)}) custom-call(f32[32,128]{1,0:T(8,128)S(1)} %get-tuple-element.51.util_ref, f32[512,128]{1,0:T(8,128)S(1)} %bitcast.57, f32[512,64]{1,0:T(8,128)S(1)} %pad_maximum_fusion.pick_ref, ...), custom_call_target="tpu_custom_call" | custom-call | tf_op jit(solution)/shard_map/pallas_call | solution.py:164
  220.4 5.8 %copy-done.8 = f32[1024,4096]{1,0:T(8,128)S(1)} copy-done((f32[1024,4096]{1,0:T(8,128)S(1)}, f32[1024,4096]{1,0:T(8,128)}, u32[]{:S(2)}) %copy-start.8) | copy-done | bytes 16777240
  228.6 19.0 %all_to_all.71 = f32[64,8,128]{2,1,0:T(8,128)S(1)} all-to-all(f32[64,8,128]{2,1,0:T(8,128)S(1)} %bitcast.62), channel_id=1, replica_groups=mesh['imp'=64,'ad'=4] {'imp'}, dimensions={0} | all-to-all | bytes 524288 | tf_op jit(solution)/shard_map/all_to_all | solution.py:270
  247.5 5.8 %copy-done.3 = f32[1024,4096]{1,0:T(8,128)S(1)} copy-done((f32[1024,4096]{1,0:T(8,128)S(1)}, f32[1024,4096]{1,0:T(8,128)}, u32[]{:S(2)}) %copy-start.3) | copy-done | bytes 16777240
  253.3 9.0 %shard_map.67 = (f32[1024,4096]{1,0:T(8,128)S(1)}, f32[16,128]{1,0:T(8,128)S(1)}, f32[32,128]{1,0:T(8,128)S(1)}) custom-call(f32[32,128]{1,0:T(8,128)S(1)} %get-tuple-element.55.util_ref, f32[512,128]{1,0:T(8,128)S(1)} %bitcast.59, f32[512,32]{1,0:T(8,128)S(1)} %fusion.1.pick_ref, f32[32,128]{1,0:T(8,128)S(1)} %get-tuple-element.74.extra_ref, ...), custom_call_target="tpu_custom_call" | custom-call | tf_op jit(solution)/shard_map/pallas_call | solution.py:164
  276.5 5.8 %copy-done.10 = f32[1024,4096]{1,0:T(8,128)S(1)} copy-done((f32[1024,4096]{1,0:T(8,128)S(1)}, f32[1024,4096]{1,0:T(8,128)}, u32[]{:S(2)}) %copy-start.10) | copy-done | bytes 16777240
  284.6 19.0 %all_to_all.72 = f32[64,8,128]{2,1,0:T(8,128)S(1)} all-to-all(f32[64,8,128]{2,1,0:T(8,128)S(1)} %bitcast.61), channel_id=1, replica_groups=mesh['imp'=64,'ad'=4] {'imp'}, dimensions={0} | all-to-all | bytes 524288 | tf_op jit(solution)/shard_map/all_to_all | solution.py:270
  303.6 5.8 %copy-done.4 = f32[1024,4096]{1,0:T(8,128)S(1)} copy-done((f32[1024,4096]{1,0:T(8,128)S(1)}, f32[1024,4096]{1,0:T(8,128)}, u32[]{:S(2)}) %copy-start.4) | copy-done | bytes 16777240
  309.4 9.0 %shard_map.69 = (f32[1024,4096]{1,0:T(8,128)S(1)}, f32[16,128]{1,0:T(8,128)S(1)}, f32[32,128]{1,0:T(8,128)S(1)}) custom-call(f32[32,128]{1,0:T(8,128)S(1)} %get-tuple-element.61.util_ref, f32[512,128]{1,0:T(8,128)S(1)} %bitcast.58, f32[512,32]{1,0:T(8,128)S(1)} %fusion.1.pick_ref, f32[32,128]{1,0:T(8,128)S(1)} %get-tuple-element.75.extra_ref, ...), custom_call_target="tpu_custom_call" | custom-call | tf_op jit(solution)/shard_map/pallas_call | solution.py:164
  318.4 6.7 %all_to_all.73.all_ref = f32[4,16,128]{2,1,0:T(8,128)S(1)} all-to-all(f32[4,16,128]{2,1,0:T(8,128)S(1)} %broadcast_in_dim.27), channel_id=1, replica_groups=mesh['imp'=64,'ad'=4] {'ad'}, dimensions={0} | all-to-all | bytes 65536 | tf_op jit(solution)/shard_map/all_to_all | solution.py:270
  328.4 7.2 %all-to-all-start.13 = ((f32[64,2,256]{2,1,0:T(2,128)}), f32[64,2,256]{2,1,0:T(2,128)S(1)}, u32[]{:S(2)}, u32[]{:S(2)}) async-start(f32[64,2,256]{2,1,0:T(2,128)} %reshape.257), calls=%async_computation.13 | async-start | bytes 262144 | tf_op jit(solution)/shard_map/all_to_all | solution.py:270
  336.3 9.7 %all-to-all-done.13 = f32[64,2,256]{2,1,0:T(2,128)S(1)} async-done(((f32[64,2,256]{2,1,0:T(2,128)}), f32[64,2,256]{2,1,0:T(2,128)S(1)}, u32[]{:S(2)}, u32[]{:S(2)}) %all-to-all-start.13) | async-done | bytes 131104 | tf_op jit(solution)/shard_map/all_to_all | solution.py:270
  (92 shorter events, 96.0 us)
Async XLA Ops:
  0.6 99.3 %copy-start.13 = (s32[1,1,32]{2,1,0:T(1,128)S(1)}, s32[1,1,32]{2,1,0:T(1,128)}, u32[]{:S(2)}) copy-start(s32[1,1,32]{2,1,0:T(1,128)} %param.13) | copy-start | bytes 388
  0.6 113.6 %copy-start.11 = (bf16[1024,128]{1,0:T(8,128)(2,1)S(1)}, bf16[1024,128]{1,0:T(8,128)(2,1)}, u32[]{:S(2)}) copy-start(bf16[1024,128]{1,0:T(8,128)(2,1)} %x_ref.1) | copy-start | bytes 786436
  2.0 22.4 %all-to-all-start.3 = ((s32[64,1,32]{2,1,0:T(1,128)}), s32[64,1,32]{2,1,0:T(1,128)S(1)}, u32[]{:S(2)}, u32[]{:S(2)}) async-start(s32[64,1,32]{2,1,0:T(1,128)} %broadcast_in_dim.21), calls=%async_computation.3 | async-start | bytes 65536 | tf_op jit(solution)/shard_map/all_to_all | solution.py:270
  24.4 46.2 %all-to-all-start.4 = ((bf16[64,48,256]{2,1,0:T(8,128)(2,1)}), bf16[64,48,256]{2,1,0:T(8,128)(2,1)S(1)}, u32[]{:S(2)}, u32[]{:S(2)}) async-start(bf16[64,48,256]{2,1,0:T(8,128)(2,1)} %reshape.242), calls=%async_computation.4 | async-start | bytes 3145728 | tf_op jit(solution)/shard_map/all_to_all | solution.py:270
  79.6 34.7 %all-to-all-start.5 = ((bf16[64,32,256]{2,1,0:T(8,128)(2,1)}), bf16[64,32,256]{2,1,0:T(8,128)(2,1)S(1)}, u32[]{:S(2)}, u32[]{:S(2)}) async-start(bf16[64,32,256]{2,1,0:T(8,128)(2,1)} %bitcast.9), calls=%async_computation.5 | async-start | bytes 2097152 | tf_op jit(solution)/shard_map/all_to_all | solution.py:270
  114.2 48.8 %copy-start.12 = (f32[6144]{0:T(1024)S(1)}, f32[6144]{0:T(1024)}, u32[]{:S(2)}) copy-start(f32[6144]{0:T(1024)} %param.12) | copy-start | bytes 73732
  126.7 5.7 %copy-start = (f32[1024,4096]{1,0:T(8,128)}, f32[1024,4096]{1,0:T(8,128)S(1)}, u32[]{:S(2)}) copy-start(f32[1024,4096]{1,0:T(8,128)S(1)} %shard_map.62.v_ref) | copy-start | bytes 50331652
  132.4 5.8 %copy-start.1 = (f32[1024,4096]{1,0:T(8,128)S(1)}, f32[1024,4096]{1,0:T(8,128)}, u32[]{:S(2)}) copy-start(f32[1024,4096]{1,0:T(8,128)} %copy-done) | copy-start | bytes 50331652
  146.9 5.7 %copy-start.5 = (f32[1024,4096]{1,0:T(8,128)}, f32[1024,4096]{1,0:T(8,128)S(1)}, u32[]{:S(2)}) copy-start(f32[1024,4096]{1,0:T(8,128)S(1)} %get-tuple-element.50.ev_ref) | copy-start | bytes 50331652
  153.3 8.6 %all-to-all-start.6 = ((f32[4,24,128]{2,1,0:T(8,128)}), f32[4,24,128]{2,1,0:T(8,128)S(1)}, u32[]{:S(2)}, u32[]{:S(2)}) async-start(f32[4,24,128]{2,1,0:T(8,128)} %broadcast_in_dim.23), calls=%async_computation.6 | async-start | bytes 98304 | tf_op jit(solution)/shard_map/all_to_all | solution.py:270
  163.1 5.8 %copy-start.6 = (f32[1024,4096]{1,0:T(8,128)S(1)}, f32[1024,4096]{1,0:T(8,128)}, u32[]{:S(2)}) copy-start(f32[1024,4096]{1,0:T(8,128)} %copy-done.5) | copy-start | bytes 50331652
  172.2 19.5 %all-to-all-start.7 = ((f32[64,8,128]{2,1,0:T(8,128)}), f32[64,8,128]{2,1,0:T(8,128)S(1)}, u32[]{:S(2)}, u32[]{:S(2)}) async-start(f32[64,8,128]{2,1,0:T(8,128)} %bitcast.16), calls=%async_computation.7 | async-start | bytes 524288 | tf_op jit(solution)/shard_map/all_to_all | solution.py:270
  191.7 5.8 %copy-start.2 = (f32[1024,4096]{1,0:T(8,128)S(1)}, f32[1024,4096]{1,0:T(8,128)}, u32[]{:S(2)}) copy-start(f32[1024,4096]{1,0:T(8,128)} %copy-done) | copy-start | bytes 50331652
  206.5 5.8 %copy-start.7 = (f32[1024,4096]{1,0:T(8,128)}, f32[1024,4096]{1,0:T(8,128)S(1)}, u32[]{:S(2)}) copy-start(f32[1024,4096]{1,0:T(8,128)S(1)} %get-tuple-element.54.ev_ref) | copy-start | bytes 50331652
  212.9 7.5 %all-to-all-start.8 = ((f32[4,16,128]{2,1,0:T(8,128)}), f32[4,16,128]{2,1,0:T(8,128)S(1)}, u32[]{:S(2)}, u32[]{:S(2)}) async-start(f32[4,16,128]{2,1,0:T(8,128)} %broadcast_in_dim.25), calls=%async_computation.8 | async-start | bytes 65536 | tf_op jit(solution)/shard_map/all_to_all | solution.py:270
  220.4 5.8 %copy-start.8 = (f32[1024,4096]{1,0:T(8,128)S(1)}, f32[1024,4096]{1,0:T(8,128)}, u32[]{:S(2)}) copy-start(f32[1024,4096]{1,0:T(8,128)} %copy-done.7) | copy-start | bytes 50331652
  247.5 5.8 %copy-start.3 = (f32[1024,4096]{1,0:T(8,128)S(1)}, f32[1024,4096]{1,0:T(8,128)}, u32[]{:S(2)}) copy-start(f32[1024,4096]{1,0:T(8,128)} %copy-done) | copy-start | bytes 50331652
  262.3 5.8 %copy-start.9 = (f32[1024,4096]{1,0:T(8,128)}, f32[1024,4096]{1,0:T(8,128)S(1)}, u32[]{:S(2)}) copy-start(f32[1024,4096]{1,0:T(8,128)S(1)} %get-tuple-element.60.ev_ref) | copy-start | bytes 50331652
  268.7 7.8 %all-to-all-start.10 = ((f32[4,16,128]{2,1,0:T(8,128)}), f32[4,16,128]{2,1,0:T(8,128)S(1)}, u32[]{:S(2)}, u32[]{:S(2)}) async-start(f32[4,16,128]{2,1,0:T(8,128)} %broadcast_in_dim.26), calls=%async_computation.10 | async-start | bytes 65536 | tf_op jit(solution)/shard_map/all_to_all | solution.py:270
  276.5 5.8 %copy-start.10 = (f32[1024,4096]{1,0:T(8,128)S(1)}, f32[1024,4096]{1,0:T(8,128)}, u32[]{:S(2)}) copy-start(f32[1024,4096]{1,0:T(8,128)} %copy-done.9) | copy-start | bytes 50331652
  303.6 5.8 %copy-start.4 = (f32[1024,4096]{1,0:T(8,128)S(1)}, f32[1024,4096]{1,0:T(8,128)}, u32[]{:S(2)}) copy-start(f32[1024,4096]{1,0:T(8,128)} %copy-done) | copy-start | bytes 50331652
  328.4 17.5 %all-to-all-start.13 = ((f32[64,2,256]{2,1,0:T(2,128)}), f32[64,2,256]{2,1,0:T(2,128)S(1)}, u32[]{:S(2)}, u32[]{:S(2)}) async-start(f32[64,2,256]{2,1,0:T(2,128)} %reshape.257), calls=%async_computation.13 | async-start | bytes 262144 | tf_op jit(solution)/shard_map/all_to_all | solution.py:270

commit v2 on v1

v2 whole, which is shorter than its diff:
```python
import functools
import math

import jax
import jax.numpy as jnp
from jax import lax
from jax.experimental import pallas as pl
from jax.experimental.pallas import tpu as pltpu
from jax.sharding import PartitionSpec as P

BLOCK = 128
ROUNDS = 4
CAP = 2
SHARED = 6

softness_level = 0.5
util_floor = 0.01
pacing_cap = 3.0

LOG2E = math.log2(math.e)
LN2 = math.log(2.0)
SCALE = LOG2E / softness_level
HI = lax.Precision.HIGHEST
f32 = jnp.float32
bf16 = jnp.bfloat16
VMEM = pl.BlockSpec(memory_space=pltpu.VMEM)


def params(mib):
    return pltpu.CompilerParams(vmem_limit_bytes=mib * 2**20)


def pinned(x):
    return pltpu.with_memory_space_constraint(x, pltpu.VMEM)


def tn(a, b):
    return lax.dot_general(a, b, (((0,), (0,)), ((), ())), precision=HI, preferred_element_type=f32)


def nn(a, b):
    return lax.dot_general(a, b, (((1,), (0,)), ((), ())), precision=HI, preferred_element_type=f32)


def eye():
    return lax.broadcasted_iota(jnp.int32, (128, 128), 0) == lax.broadcasted_iota(
        jnp.int32, (128, 128), 1
    )


def spread_kernel(x_ref, out_ref, rows):
    half = out_ref.shape[0]
    own = out_ref.shape[1]
    rows[...] = x_ref[...].astype(f32)

    def one(p, _):
        for side in range(2):
            part = rows[pl.ds(p + side * half, own, stride=BLOCK), :]
            out_ref[p, :, side * 128 : (side + 1) * 128] = part.astype(bf16)
        return 0

    lax.fori_loop(0, half, one, 0)


def spread_call(ad_vectors):
    own = ad_vectors.shape[0] // BLOCK
    return pl.pallas_call(
        spread_kernel,
        out_shape=jax.ShapeDtypeStruct((BLOCK // 2, own, 256), bf16),
        in_specs=[VMEM],
        out_specs=VMEM,
        scratch_shapes=[pltpu.VMEM(ad_vectors.shape, f32)],
        compiler_params=params(24),
    )(ad_vectors)


def finish_score(v_ref, ev_ref, ms_ref, pace, sums, tops, highest):
    rows = v_ref.shape[0]
    chunks = rows // 128
    ms_ref[:, 0:chunks, :] = jnp.zeros((ms_ref.shape[0], chunks, 128), f32)

    @pl.when(jnp.logical_not(jnp.max(highest) < 2.0**90))
    def _():
        def body(step, _):
            at = pl.ds(pl.multiple_of(step * 8, 8), 8)
            v = v_ref[at, :]
            t = v * pace[...]
            m = jnp.max(t, axis=1, keepdims=True)
            e = jnp.exp2(t - m)
            ev_ref[at, :] = e * v
            tops[at, :] = jnp.broadcast_to(m, (8, 128))
            lane = lax.broadcasted_iota(jnp.int32, (8, 128), 1)
            sums[at, :] = jnp.where(lane == 0, jnp.sum(e, axis=1, keepdims=True), 0.0)
            return 0

        lax.fori_loop(0, rows // 8, body, 0)
        for c in range(chunks):
            row = jnp.sum(jnp.where(eye(), tops[c * 128 : (c + 1) * 128, :], 0.0), axis=0, keepdims=True)
            for a in range(ms_ref.shape[0]):
                ms_ref[a, c : c + 1, :] = row

    total = lax.dot_general(
        jnp.ones((8, 128), f32), sums[...], (((1,), (1,)), ((), ())), precision=HI, preferred_element_type=f32
    )
    for c in range(chunks):
        for a in range(ms_ref.shape[0]):
            ms_ref[a, chunks + c : chunks + c + 1, :] = total[0:1, c * 128 : (c + 1) * 128]


def values_kernel(blocks, x_ref, y_ref, v_ref, ev_ref, ms_ref, ya, yb, yt, pace, sums, tops):
    parts = y_ref.shape[0] // blocks
    ya[...] = y_ref[:, :128].astype(f32)
    yb[...] = y_ref[:, 128:].astype(f32)

    def unpack(k, _):
        at = pl.multiple_of(k * BLOCK, BLOCK)
        yt[pl.ds(at, parts), :] = ya[pl.ds(k, parts, stride=blocks), :].astype(bf16)
        yt[pl.ds(at + parts, parts), :] = yb[pl.ds(k, parts, stride=blocks), :].astype(bf16)
        return 0

    lax.fori_loop(0, blocks, unpack, 0)
    rows = x_ref.shape[0]
    tile_c = 1024
    sums[...] = jnp.zeros(sums.shape, f32)

    def tile(step, _):
        cols = pl.ds(pl.multiple_of(step * tile_c, tile_c), tile_c)
        s = lax.dot_general(
            x_ref[...], yt[cols, :], (((1,), (1,)), ((), ())), preferred_element_type=f32
        )
        v = jnp.maximum(s, 0.0) + jnp.log(1.0 + jnp.exp2(jnp.abs(s) * -LOG2E))
        e = jnp.exp2(v * SCALE)
        v_ref[:, cols] = v
        ev_ref[:, cols] = e * v
        part = e[:, 0:128]
        for k in range(1, tile_c // 128):
            part = part + e[:, k * 128 : (k + 1) * 128]
        sums[...] += part
        return 0

    lax.fori_loop(0, v_ref.shape[1] // tile_c, tile, 0)
    pace[...] = jnp.full(pace.shape, SCALE, f32)
    highest = jnp.max(sums[...].reshape(rows // 8, 8, 128), axis=0)
    finish_score(v_ref, ev_ref, ms_ref, pace, sums, tops, highest)


def score_scratch(rows, width):
    return [pltpu.VMEM((8, width), f32), pltpu.VMEM((rows, 128), f32), pltpu.VMEM((rows, 128), f32)]


def values_call(x, y, blocks, columns):
    rows, width = x.shape[0], blocks * BLOCK
    return pl.pallas_call(
        functools.partial(values_kernel, blocks),
        out_shape=[
            pltpu.VMEM((rows, width), f32),
            pltpu.VMEM((rows, width), f32),
            jax.ShapeDtypeStruct((columns, rows // 64, 128), f32),
        ],
        in_specs=[VMEM, VMEM],
        out_specs=[VMEM] * 3,
        scratch_shapes=[
            pltpu.VMEM((y.shape[0], 128), f32),
            pltpu.VMEM((y.shape[0], 128), f32),
            pltpu.VMEM((width, 128), bf16),
        ]
        + score_scratch(rows, width),
        compiler_params=params(24),
    )(x, y)


def score(v_ref, ev_ref, ms_ref, pace, sums, tops):
    rows, width = v_ref.shape
    step_rows = 128

    def body(step, highest):
        base = pl.multiple_of(step * step_rows, step_rows)
        total = [None] * (step_rows // 8)
        for k in range(width // 128):
            cols = slice(k * 128, (k + 1) * 128)
            scale = pace[:, cols]
            for part in range(step_rows // 8):
                v = v_ref[pl.ds(base + part * 8, 8), cols]
                e = jnp.exp2(v * scale)
                ev_ref[pl.ds(base + part * 8, 8), cols] = e * v
                total[part] = e if k == 0 else total[part] + e
        for part in range(step_rows // 8):
            sums[pl.ds(base + part * 8, 8), :] = total[part]
            highest = jnp.maximum(highest, total[part])
        return highest

    highest = lax.fori_loop(0, rows // step_rows, body, jnp.zeros((8, 128), f32))
    finish_score(v_ref, ev_ref, ms_ref, pace, sums, tops, highest)


def pace_step(pace, util, limit):
    return jnp.sqrt(pace * jnp.minimum(limit / jnp.maximum(util, util_floor), pacing_cap))


def spread_pace(p, pace):
    for k in range(p.shape[0]):
        pace[:, k * BLOCK : (k + 1) * BLOCK] = jnp.broadcast_to(p[k : k + 1, :] * SCALE, (8, BLOCK))


def second_score_kernel(
    util_ref, recv_ref, pick_ref, v_in, ev_in, v_ref, ev_ref, ms_ref, p_ref, limit_ref, pace, sums, tops
):
    blocks = util_ref.shape[0]
    got = tn(pick_ref[...], recv_ref[...].reshape(-1, BLOCK))
    limit = got[blocks:, :]
    p = pace_step(jnp.ones(limit.shape, f32), util_ref[...] + got[:blocks, :], limit)
    p_ref[...] = p
    limit_ref[...] = limit
    spread_pace(p, pace)
    score(v_in, ev_ref, ms_ref, pace, sums, tops)


def score_kernel(
    util_ref, recv_ref, pick_ref, limit_ref, old_ref, v_in, ev_in, v_ref, ev_ref, ms_ref, p_ref, pace, sums, tops
):
    util = util_ref[...] + tn(pick_ref[...], recv_ref[...].reshape(-1, BLOCK))
    p = pace_step(old_ref[...], util, limit_ref[...])
    p_ref[...] = p
    spread_pace(p, pace)
    score(v_in, ev_ref, ms_ref, pace, sums, tops)


def score_call(kernel, v, ev, args, columns, outs):
    rows, width = v.shape
    small = jax.ShapeDtypeStruct((width // BLOCK, BLOCK), f32)
    return pl.pallas_call(
        kernel,
        out_shape=[
            pltpu.VMEM((rows, width), f32),
            pltpu.VMEM((rows, width), f32),
            jax.ShapeDtypeStruct((columns, rows // 64, 128), f32),
        ]
        + [small] * outs,
        in_specs=[VMEM] * (len(args) + 2),
        out_specs=[VMEM] * (3 + outs),
        scratch_shapes=score_scratch(rows, width),
        input_output_aliases={len(args): 0, len(args) + 1: 1},
        compiler_params=params(24),
    )(*args, pinned(v), pinned(ev))


def combine(ms_ref, all_ref):
    chunks = ms_ref.shape[1] // 2
    tops = all_ref[:, 0:chunks, :]
    sums = all_ref[:, chunks : 2 * chunks, :]
    top = jnp.max(tops, axis=0)
    total = jnp.sum(sums * jnp.exp2(tops - top[None]), axis=0)
    lse = top + LOG2E * jnp.log(total)
    return lse, jnp.exp2(ms_ref[0, 0:chunks, :] - lse)


def utility(weight, ev_ref, util_ref, wcol):
    rows, width = ev_ref.shape
    for c in range(rows // 128):
        spread = jnp.where(eye(), jnp.broadcast_to(weight[c : c + 1, :], (128, 128)), 0.0)
        wcol[c * 128 : (c + 1) * 128, :] = jnp.broadcast_to(
            jnp.sum(spread, axis=1, keepdims=True), (128, 128)
        )
    blocks = width // BLOCK
    step_rows = 128

    def body(step, acc):
        out = list(acc)
        base = pl.multiple_of(step * step_rows, step_rows)
        for part in range(step_rows // 8):
            at = pl.ds(base + part * 8, 8)
            w = wcol[at, :]
            for k in range(blocks):
                out[k] = out[k] + ev_ref[at, k * BLOCK : (k + 1) * BLOCK] * w
        return tuple(out)

    acc = lax.fori_loop(
        0, rows // step_rows, body, tuple(jnp.zeros((8, BLOCK), f32) for _ in range(blocks))
    )
    for k in range(blocks):
        util_ref[k : k + 1, :] = jnp.sum(acc[k], axis=0, keepdims=True)


def utility_kernel(first, ms_ref, all_ref, put_ref, *refs):
    refs = list(refs)
    if first:
        own_put_ref, limit_ref = refs[:2]
        refs = refs[2:]
    v_in, ev_in, v_ref, ev_ref, util_ref, send_ref, wcol = refs
    _, weight = combine(ms_ref, all_ref)
    utility(weight, ev_in, util_ref, wcol)
    send = nn(put_ref[...], util_ref[...])
    if first:
        send = send + nn(own_put_ref[...], limit_ref[...])
    send_ref[...] = send.reshape(send_ref.shape)


def last_utility_kernel(ms_ref, all_ref, put_ref, p_ref, v_in, ev_in, v_ref, ev_ref, both_ref, send_ref, price_ref, wcol):
    lse, weight = combine(ms_ref, all_ref)
    price_ref[...] = lse * (softness_level * LN2)
    blocks = p_ref.shape[0]
    utility(weight, ev_in, both_ref, wcol)
    both_ref[blocks:, :] = p_ref[...]
    send_ref[...] = nn(put_ref[...], both_ref[...]).reshape(send_ref.shape)


def utility_call(kernel, v, ev, args, util_rows, send_shape, price):
    rows, width = ev.shape
    outs = [
        pltpu.VMEM((rows, width), f32),
        pltpu.VMEM((rows, width), f32),
        jax.ShapeDtypeStruct((util_rows, BLOCK), f32),
        jax.ShapeDtypeStruct(send_shape, f32),
    ]
    if price:
        outs.append(jax.ShapeDtypeStruct((rows // 128, 128), f32))
    return pl.pallas_call(
        kernel,
        out_shape=outs,
        in_specs=[VMEM] * (len(args) + 2),
        out_specs=[VMEM] * len(outs),
        scratch_shapes=[pltpu.VMEM((rows, 128), f32)],
        input_output_aliases={len(args): 0, len(args) + 1: 1},
        compiler_params=params(24),
    )(*args, pinned(v), pinned(ev))


def last_pace_kernel(recv_ref, back_ref, limit_ref, out_ref):
    limit = limit_ref[...]
    own = limit.shape[0]
    back = back_ref[...]
    got = nn(back, recv_ref[...].reshape(-1, BLOCK))
    count = jnp.sum(back[own:, :], axis=1, keepdims=True)
    lone = jnp.ones(limit.shape, f32)
    for _ in range(ROUNDS - 1):
        lone = pace_step(lone, jnp.zeros(limit.shape, f32), limit)
    pace = jnp.where(count > 0.0, got[own:, :] / jnp.maximum(count, 1.0), lone)
    out_ref[...] = pace_step(pace, got[:own, :], limit)


def before(flags, axis):
    size = flags.shape[axis]
    order = jnp.arange(size)
    less = (order[:, None] < order[None, :]).astype(f32)
    moved = jnp.moveaxis(flags, axis, -1).astype(f32)
    return jnp.moveaxis(jnp.dot(moved, less), -1, axis).astype(jnp.int32)


def swap(x, axis):
    return lax.all_to_all(x, axis, split_axis=0, concat_axis=0, tiled=True)


def share_plan(lists, wanted, equal, placed, back, shared):
    owners, size = lists.shape
    own_blocks = back.shape[2]
    gives = jnp.any(equal, axis=1)
    takes = jnp.any(equal, axis=2)
    slot = jnp.arange(shared, dtype=jnp.int32)[None, :, None]
    put = ((before(gives, 1)[:, None, :] == slot) & gives[:, None, :]).astype(f32)
    take_slot = ((before(takes, 1)[:, None, :] == slot) & takes[:, None, :]).astype(f32)
    pick = jnp.einsum("isk,ikw->isw", take_slot, equal.astype(f32))
    slots = shared + CAP

    def pad(x, low, high):
        return jnp.pad(x, ((0, 0), (low, high), (0, 0))).reshape(owners * slots, x.shape[2])

    put, pick = pad(put, 0, CAP), pad(pick, 0, CAP)
    own_put, limit_pick = pad(back, shared, 0), pad(placed, shared, 0)
    return put, pick, own_put, jnp.concatenate([pick, limit_pick], axis=1)


def rounds(columns, shared, imp_vectors, mine, limits, plan, last_put, last_back):
    put, pick, own_put, first_pick = plan
    size = put.shape[1]
    owners = put.shape[0] // (shared + CAP)
    shape = (owners, shared + CAP, BLOCK)
    v, ev, ms = values_call(imp_vectors, mine, size, columns)
    every = swap(ms, "ad")
    v, ev, util, send = utility_call(
        functools.partial(utility_kernel, True), v, ev, [ms, every, put, own_put, limits], size, shape, False
    )
    recv = swap(send, "imp")
    v, ev, ms, pace, wanted_limits = score_call(
        second_score_kernel, v, ev, [util, recv, first_pick], columns, 2
    )
    for step in range(2, ROUNDS):
        every = swap(ms, "ad")
        v, ev, util, send = utility_call(
            functools.partial(utility_kernel, False), v, ev, [ms, every, put], size, shape, False
        )
        recv = swap(send, "imp")
        v, ev, ms, pace = score_call(
            score_kernel, v, ev, [util, recv, pick, wanted_limits, pace], columns, 1
        )
    every = swap(ms, "ad")
    _, _, _, send, prices = utility_call(
        last_utility_kernel, v, ev, [ms, every, last_put, pace], 2 * size, (owners, 2 * CAP, BLOCK), True
    )
    recv = swap(send, "imp")
    final = pl.pallas_call(
        last_pace_kernel,
        out_shape=jax.ShapeDtypeStruct(limits.shape, f32),
        in_specs=[VMEM] * 3,
        out_specs=VMEM,
    )(recv, last_back, limits)
    return final, prices


def per_device(imp_vectors, ad_vectors, spend_limits, targets):
    owners = lax.axis_size("imp")
    columns = lax.axis_size("ad")
    me = lax.axis_index("imp")
    emb = imp_vectors.shape[1]
    own_blocks = ad_vectors.shape[0] // BLOCK
    wanted = targets.reshape(-1)
    size = wanted.shape[0]
    limits = spend_limits.reshape(own_blocks, BLOCK)

    lists = swap(jnp.broadcast_to(wanted[None, :], (owners, size)), "imp")
    table = swap(spread_call(ad_vectors), "imp").reshape(owners * own_blocks, 2 * emb)
    chosen = table[lists.reshape(-1)].reshape(owners, size, 2 * emb)
    mine = swap(chosen, "imp").reshape(owners * size, 2 * emb)

    peer = jnp.arange(owners, dtype=jnp.int32)
    equal = (lists[:, :, None] == wanted[None, None, :]) & (peer != me)[:, None, None]
    owner_of = wanted // own_blocks
    rank_of = jnp.sum(
        (owner_of[:, None] == owner_of[None, :]) & (jnp.arange(size)[None, :] < jnp.arange(size)[:, None]),
        axis=1,
    )
    lane = jnp.arange(CAP, dtype=jnp.int32)
    placed = (
        (owner_of[None, None, :] == peer[:, None, None]) & (rank_of[None, None, :] == lane[None, :, None])
    ).astype(f32)
    at_me = lists // own_blocks == me
    asked = (before(at_me, 1)[:, None, :] == lane[None, :, None]) & at_me[:, None, :]
    local = jnp.arange(own_blocks, dtype=jnp.int32)
    here = (lists[:, :, None] - me * own_blocks) == local[None, None, :]
    back = jnp.einsum("irk,ikl->irl", asked.astype(f32), here.astype(f32))

    def doubled(x):
        none = jnp.zeros_like(x)
        both = jnp.concatenate(
            [jnp.concatenate([x, none], axis=2), jnp.concatenate([none, x], axis=2)], axis=1
        )
        return both.reshape(owners * 2 * CAP, 2 * x.shape[2])

    last_put, last_back = doubled(placed), doubled(back).T
    narrow = share_plan(lists, wanted, equal, placed, back, SHARED)

    holds = jnp.any(
        lists[:, :, None] == jnp.arange(owners * own_blocks, dtype=jnp.int32)[None, None, :], axis=1
    ).astype(bf16)
    common = lax.dot_general(holds, holds, (((1,), (1,)), ((), ())), preferred_element_type=f32)
    crowded = jnp.any((common > SHARED + 0.5) & (peer[:, None] != peer[None, :]))
    over = lax.pmax(crowded.astype(f32), "ad") > 0.5
    mine, narrow, last_put, last_back = lax.optimization_barrier((mine, narrow, last_put, last_back))

    def take_narrow():
        return rounds(columns, SHARED, imp_vectors, mine, limits, narrow, last_put, last_back)

    def take_wide():
        plan = share_plan(lists, wanted, equal, placed, back, size)
        return rounds(columns, size, imp_vectors, mine, limits, plan, last_put, last_back)

    final, prices = lax.cond(over, take_wide, take_narrow)
    return final.reshape(-1), prices.reshape(-1)


def solution(mesh):
    return jax.shard_map(
        per_device,
        mesh=mesh,
        in_specs=(P("imp", None), P(("imp", "ad"), None), P(("imp", "ad")), P("imp", "ad", None)),
        out_specs=(P(("imp", "ad")), P("imp")),
        check_vma=False,
    )
```

time: 355 us -> 394 us (1.11)
  Pallas kernels: 60.7 us -> 160 us
  blocking collectives: 44.6 us -> 119 us
  local copies, waits for them, and re-layouts: 84.4 us -> 13.6 us
  waiting for transfers between devices: 84.8 us -> 40.2 us
  starting transfers between devices: 51.4 us -> 27 us
  loops' own time: 0.04 us -> 9.25 us
    pallas_call x10, Pallas kernels: 60.7 us -> 160 us  [the longest x3 102 us: score_call(): pl.pallas_call(kernel, out_shape=[pltpu.VMEM((rows, width), f32), pltpu.V...]
    all_to_all x3 -> x8, blocking collectives: 44.6 us -> 109 us  [swap(): return lax.all_to_all(x, axis, split_axis=0, concat_axis=0, tiled=True)]
    unnamed x28 -> x11, local copies, waits for them, and re-layouts: 63.3 us -> 2.06 us
    all_to_all x8 -> x3, waiting for transfers between devices: 84.8 us -> 40.2 us  [swap(): return lax.all_to_all(x, axis, split_axis=0, concat_axis=0, tiled=True)]
    all_to_all x8 -> x3, starting transfers between devices: 51.4 us -> 27 us  [swap(): return lax.all_to_all(x, axis, split_axis=0, concat_axis=0, tiled=True)]
    pmax x0 -> x1, blocking collectives: none -> 9.55 us  [per_device(): over = lax.pmax(crowded.astype(f32), 'ad') > 0.5]
    another operation x3 -> x1, loops' own time: 0.04 us -> 9.25 us  [per_device(): final, prices = lax.cond(over, take_wide, take_narrow)]
    reshape x5 -> x3, local copies, waits for them, and re-layouts: 4.46 us -> 0.21 us  [the longest x2 0.13 us: pad(): jnp.pad(x, ((0, 0), (low, high), (0, 0)))]
  transfers between devices with their start and end apart: 8 -> 3, of which waited for: 8 -> 3; matrix products, arithmetic and copies ran while one was open for 8% -> 5% of each run, Pallas kernels for 0% -> 1%
where the time goes in v2:
time: 394 us; the launch traced here: 390 us
  Pallas kernels  160 us (41%)
  blocking collectives  119 us (30%)
  waiting for transfers between devices  40.2 us (10%)
  starting transfers between devices  27 us (7%)
  other arithmetic  15.8 us (4%)
  local copies, waits for them, and re-layouts  13.6 us (3%)
  loops' own time  9.25 us (2%)
    all_to_all x8, blocking collectives, swap(): return lax.all_to_all(x, axis, split_axis=0, concat_axis=0, tiled=True)  109 us
    pallas_call x3, Pallas kernels, score_call(): pl.pallas_call(kernel, out_shape=[pltpu.VMEM((rows, width), f32), pltpu.V...  102 us
    all_to_all x3, waiting for transfers between devices, swap(): return lax.all_to_all(x, axis, split_axis=0, concat_axis=0, tiled=True)  40.2 us
    pallas_call x1, Pallas kernels, values_call(): pl.pallas_call(functools.partial(values_kernel, blocks), out_shape=[pltpu...  38.9 us
    all_to_all x3, starting transfers between devices, swap(): return lax.all_to_all(x, axis, split_axis=0, concat_axis=0, tiled=True)  27 us
    pallas_call x4, Pallas kernels, utility_call(): pl.pallas_call(kernel, out_shape=outs, in_specs=[VMEM] * (len(args) + 2),...  13.1 us
    reduce_or x1, other arithmetic, per_device(): jnp.any(lists[:, :, None] == jnp.arange(owners * own_blocks, dtype=jnp.in...  11 us
    pmax x1, blocking collectives, per_device(): over = lax.pmax(crowded.astype(f32), 'ad') > 0.5  9.55 us
  transfers between devices with their start and end apart: 3, of which 3 were waited for; matrix products, arithmetic and copies ran while one was open for 5% of the time, Pallas kernels for 1%

profile of v2, /device:TPU:1, one launch (start us, length us, event | category | flops | bytes accessed | tf_op | source)
XLA Modules:
  0.0 390.0 jit_solution(7383201208452093180)
XLA Ops:
  1.9 13.2 %all-to-all-start.16 = ((s32[64,1,32]{2,1,0:T(1,128)}), s32[64,1,32]{2,1,0:T(1,128)S(1)}, u32[]{:S(2)}, u32[]{:S(2)}) async-start(s32[64,1,32]{2,1,0:T(1,128)} %broadcast_in_dim.2), calls=%async_computation.16 | async-start | bytes 65536 | tf_op jit(solution)/shard_map/all_to_all | solution.py:350
  16.5 5.0 %shard_map.62 = bf16[64,48,256]{2,1,0:T(8,128)(2,1)} custom-call(bf16[6144,128]{1,0:T(8,128)(2,1)S(1)} %copy-done.8), custom_call_target="tpu_custom_call" | custom-call | tf_op jit(solution)/shard_map/pallas_call | solution.py:67
  24.4 7.7 %all-to-all-start.17 = ((bf16[64,48,256]{2,1,0:T(8,128)(2,1)}), bf16[64,48,256]{2,1,0:T(8,128)(2,1)S(1)}, u32[]{:S(2)}, u32[]{:S(2)}) async-start(bf16[64,48,256]{2,1,0:T(8,128)(2,1)} %shard_map.62), calls=%async_computation.17 | async-start | bytes 3145728 | tf_op jit(solution)/shard_map/all_to_all | solution.py:350
  35.2 11.0 %fusion.6 = pred[64,3072]{1,0:T(8,128)(4,1)S(1)} fusion(s32[64,32]{1,0:T(8,128)S(1)} %bitcast.47), kind=kLoop, calls=%fused_computation.14 | loop fusion | flops 12386304 | bytes 204800 | tf_op jit(solution)/shard_map/reduce_or | solution.py:451
  50.4 21.3 %all-to-all-done.17 = bf16[64,48,256]{2,1,0:T(8,128)(2,1)S(1)} async-done(((bf16[64,48,256]{2,1,0:T(8,128)(2,1)}), bf16[64,48,256]{2,1,0:T(8,128)(2,1)S(1)}, u32[]{:S(2)}, u32[]{:S(2)}) %all-to-all-start.17) | async-done | bytes 1572896 | tf_op jit(solution)/shard_map/all_to_all | solution.py:350
  71.7 9.0 %gather_fusion = bf16[2048,256]{1,0:T(8,128)(2,1)} fusion(bf16[3072,256]{1,0:T(8,128)(2,1)S(1)} %bitcast.41, s32[2048]{0:T(1024)S(1)} %broadcast_clamp_fusion), kind=kCustom, calls=%fused_computation | custom fusion | bytes 2105344 | tf_op jit(solution)/shard_map/gather | solution.py:421
  80.7 6.1 %all-to-all-start.18 = ((bf16[64,32,256]{2,1,0:T(8,128)(2,1)}), bf16[64,32,256]{2,1,0:T(8,128)(2,1)S(1)}, u32[]{:S(2)}, u32[]{:S(2)}) async-start(bf16[64,32,256]{2,1,0:T(8,128)(2,1)} %bitcast.6), calls=%async_computation.18 | async-start | bytes 2097152 | tf_op jit(solution)/shard_map/all_to_all | solution.py:350
  87.0 9.6 %pmax.7 = f32[]{:T(128)} all-reduce(f32[]{:T(128)S(6)} %convert_element_type.29), channel_id=1, replica_groups=mesh['imp'=64,'ad'=4] {'ad'}, use_global_device_ids=true, to_apply=%region_2.3 | all-reduce | flops 1 | bytes 8 | tf_op jit(solution)/shard_map/pmax | solution.py:456
  99.3 16.0 %all-to-all-done.18 = bf16[64,32,256]{2,1,0:T(8,128)(2,1)S(1)} async-done(((bf16[64,32,256]{2,1,0:T(8,128)(2,1)}), bf16[64,32,256]{2,1,0:T(8,128)(2,1)S(1)}, u32[]{:S(2)}, u32[]{:S(2)}) %all-to-all-start.18) | async-done | bytes 1048608 | tf_op jit(solution)/shard_map/all_to_all | solution.py:350
  115.3 273.5 %conditional.1 = (f32[8,128]{1,0:T(8,128)S(1)}, f32[6144]{0:T(1024)S(1)}) conditional(s32[]{:T(128)} %convert_element_type.30, (bf16[1024,128]{1,0:T(8,128)(2,1)S(1)}, bf16[2048,256]{1,0:T(8,128)(2,1)S(1)}, f32[512,32]{1,0:T(8,128)S(1)}, f32[512,48]{1,0:T(8,128)S(1)}, f32[48,128]{1,0:T(8,128)S(1)}, /*index=5*/f32[512,64]{1,0:T(8,128)S(1)}, ...), branch_computations={%region_6.7_spmd, %region_7.10_spmd} | conditional | flops 5060608 | bytes 560628096 | solution.py:466
  115.3 38.9 %branch_0_fun.9 = (f32[1024,4096]{1,0:T(8,128)S(1)}, f32[1024,4096]{1,0:T(8,128)S(1)}, f32[4,16,128]{2,1,0:T(8,128)}) custom-call(bf16[1024,128]{1,0:T(8,128)(2,1)S(1)} %get-tuple-element.35.x_ref, bf16[2048,256]{1,0:T(8,128)(2,1)S(1)} %get-tuple-element.36.y_ref), custom_call_target="tpu_custom_call" | custom-call | tf_op jit(solution)/shard_map/cond/branch_0_fun/pallas_call | solution.py:153
  154.3 8.4 %all_to_all.80.all_ref = f32[4,16,128]{2,1,0:T(8,128)} all-to-all(f32[4,16,128]{2,1,0:T(8,128)} %get-tuple-element.37.ms_ref), channel_id=1, replica_groups=mesh['imp'=64,'ad'=4] {'ad'}, dimensions={0} | all-to-all | bytes 65536 | tf_op jit(solution)/shard_map/cond/branch_0_fun/all_to_all | solution.py:350
  162.7 3.5 branch_0_fun.10
  166.2 19.7 %all_to_all.81.recv_ref = f32[64,8,128]{2,1,0:T(8,128)} all-to-all(f32[64,8,128]{2,1,0:T(8,128)} %get-tuple-element.44), channel_id=1, replica_groups=mesh['imp'=64,'ad'=4] {'imp'}, dimensions={0} | all-to-all | bytes 524288 | tf_op jit(solution)/shard_map/cond/branch_0_fun/all_to_all | solution.py:350
  185.9 34.0 %branch_0_fun.11 = (f32[1024,4096]{1,0:T(8,128)S(1)}, f32[1024,4096]{1,0:T(8,128)S(1)}, f32[4,16,128]{2,1,0:T(8,128)}, f32[32,128]{1,0:T(8,128)}, f32[32,128]{1,0:T(8,128)}) custom-call(f32[32,128]{1,0:T(8,128)} %get-tuple-element.43.util_ref, f32[64,8,128]{2,1,0:T(8,128)} %all_to_all.81.recv_ref, ...), custom_call_target="tpu_custom_call", output_to_operand_aliasing={{0}: (3, {}), {1}: (4, {})} | custom-call | tf_op jit(solution)/shard_map/cond/branch_0_fun/pallas_call | solution.py:231
  219.9 8.2 %all_to_all.82.all_ref = f32[4,16,128]{2,1,0:T(8,128)} all-to-all(f32[4,16,128]{2,1,0:T(8,128)} %get-tuple-element.48.ms_ref), channel_id=1, replica_groups=mesh['imp'=64,'ad'=4] {'ad'}, dimensions={0} | all-to-all | bytes 65536 | tf_op jit(solution)/shard_map/cond/branch_0_fun/all_to_all | solution.py:350
  228.2 3.3 branch_0_fun.12
  231.4 19.3 %all_to_all.83.recv_ref = f32[64,8,128]{2,1,0:T(8,128)} all-to-all(f32[64,8,128]{2,1,0:T(8,128)} %get-tuple-element.52), channel_id=1, replica_groups=mesh['imp'=64,'ad'=4] {'imp'}, dimensions={0} | all-to-all | bytes 524288 | tf_op jit(solution)/shard_map/cond/branch_0_fun/all_to_all | solution.py:350
  250.7 34.0 %branch_0_fun.13 = (f32[1024,4096]{1,0:T(8,128)S(1)}, f32[1024,4096]{1,0:T(8,128)S(1)}, f32[4,16,128]{2,1,0:T(8,128)}, f32[32,128]{1,0:T(8,128)}) custom-call(f32[32,128]{1,0:T(8,128)} %get-tuple-element.51.util_ref, f32[64,8,128]{2,1,0:T(8,128)} %all_to_all.83.recv_ref, ...), custom_call_target="tpu_custom_call", output_to_operand_aliasing={{0}: (5, {}), {1}: (6, {})} | custom-call | tf_op jit(solution)/shard_map/cond/branch_0_fun/pallas_call | solution.py:231
  284.7 8.2 %all_to_all.84.all_ref = f32[4,16,128]{2,1,0:T(8,128)} all-to-all(f32[4,16,128]{2,1,0:T(8,128)} %get-tuple-element.58.ms_ref), channel_id=1, replica_groups=mesh['imp'=64,'ad'=4] {'ad'}, dimensions={0} | all-to-all | bytes 65536 | tf_op jit(solution)/shard_map/cond/branch_0_fun/all_to_all | solution.py:350
  296.2 19.3 %all_to_all.85.recv_ref = f32[64,8,128]{2,1,0:T(8,128)} all-to-all(f32[64,8,128]{2,1,0:T(8,128)} %get-tuple-element.62), channel_id=1, replica_groups=mesh['imp'=64,'ad'=4] {'imp'}, dimensions={0} | all-to-all | bytes 524288 | tf_op jit(solution)/shard_map/cond/branch_0_fun/all_to_all | solution.py:350
  315.5 34.0 %branch_0_fun.15 = (f32[1024,4096]{1,0:T(8,128)S(1)}, f32[1024,4096]{1,0:T(8,128)S(1)}, f32[4,16,128]{2,1,0:T(8,128)}, f32[32,128]{1,0:T(8,128)}) custom-call(f32[32,128]{1,0:T(8,128)} %get-tuple-element.61.util_ref, f32[64,8,128]{2,1,0:T(8,128)} %all_to_all.85.recv_ref, ...), custom_call_target="tpu_custom_call", output_to_operand_aliasing={{0}: (5, {}), {1}: (6, {})} | custom-call | tf_op jit(solution)/shard_map/cond/branch_0_fun/pallas_call | solution.py:231
  349.5 8.2 %all_to_all.86.all_ref = f32[4,16,128]{2,1,0:T(8,128)} all-to-all(f32[4,16,128]{2,1,0:T(8,128)} %get-tuple-element.66.ms_ref), channel_id=1, replica_groups=mesh['imp'=64,'ad'=4] {'ad'}, dimensions={0} | all-to-all | bytes 65536 | tf_op jit(solution)/shard_map/cond/branch_0_fun/all_to_all | solution.py:350
  360.8 17.6 %all_to_all.87.recv_ref = f32[64,4,128]{2,1,0:T(4,128)} all-to-all(f32[64,4,128]{2,1,0:T(4,128)} %get-tuple-element.72), channel_id=1, replica_groups=mesh['imp'=64,'ad'=4] {'imp'}, dimensions={0} | all-to-all | bytes 262144 | tf_op jit(solution)/shard_map/cond/branch_0_fun/all_to_all | solution.py:350
  (51 shorter events, 22.1 us)
Async XLA Ops:
  0.6 114.7 %copy-start.16 = (f32[6144]{0:T(1024)S(1)}, f32[6144]{0:T(1024)}, u32[]{:S(2)}) copy-start(f32[6144]{0:T(1024)} %param.8) | copy-start | bytes 73732
  1.9 22.4 %all-to-all-start.16 = ((s32[64,1,32]{2,1,0:T(1,128)}), s32[64,1,32]{2,1,0:T(1,128)S(1)}, u32[]{:S(2)}, u32[]{:S(2)}) async-start(s32[64,1,32]{2,1,0:T(1,128)} %broadcast_in_dim.2), calls=%async_computation.16 | async-start | bytes 65536 | tf_op jit(solution)/shard_map/all_to_all | solution.py:350
  15.1 1.4 copy-start.8
  16.5 98.8 %copy-start.13 = (bf16[1024,128]{1,0:T(8,128)(2,1)S(1)}, bf16[1024,128]{1,0:T(8,128)(2,1)}, u32[]{:S(2)}) copy-start(bf16[1024,128]{1,0:T(8,128)(2,1)} %param.6) | copy-start | bytes 786436
  24.4 47.3 %all-to-all-start.17 = ((bf16[64,48,256]{2,1,0:T(8,128)(2,1)}), bf16[64,48,256]{2,1,0:T(8,128)(2,1)S(1)}, u32[]{:S(2)}, u32[]{:S(2)}) async-start(bf16[64,48,256]{2,1,0:T(8,128)(2,1)} %shard_map.62), calls=%async_computation.17 | async-start | bytes 3145728 | tf_op jit(solution)/shard_map/all_to_all | solution.py:350
  80.7 34.7 %all-to-all-start.18 = ((bf16[64,32,256]{2,1,0:T(8,128)(2,1)}), bf16[64,32,256]{2,1,0:T(8,128)(2,1)S(1)}, u32[]{:S(2)}, u32[]{:S(2)}) async-start(bf16[64,32,256]{2,1,0:T(8,128)(2,1)} %bitcast.6), calls=%async_computation.18 | async-start | bytes 2097152 | tf_op jit(solution)/shard_map/all_to_all | solution.py:350
  388.9 0.6 copy-start.20
  388.9 0.6 copy-start.21

commit v3 on v2

v3 whole, which is shorter than its diff:
```python
import functools
import math

import jax
import jax.numpy as jnp
from jax import lax
from jax.experimental import pallas as pl
from jax.experimental.pallas import tpu as pltpu
from jax.sharding import PartitionSpec as P

BLOCK = 128
ROUNDS = 4
CAP = 2
SHARED = 6

softness_level = 0.5
util_floor = 0.01
pacing_cap = 3.0

LOG2E = math.log2(math.e)
LN2 = math.log(2.0)
SCALE = LOG2E / softness_level
SAFE = 2.0**90
HI = lax.Precision.HIGHEST
f32 = jnp.float32
bf16 = jnp.bfloat16
VMEM = pl.BlockSpec(memory_space=pltpu.VMEM)
SMEM = pl.BlockSpec(memory_space=pltpu.SMEM)


def params():
    return pltpu.CompilerParams(vmem_limit_bytes=24 * 2**20)


def pinned(x):
    return pltpu.with_memory_space_constraint(x, pltpu.VMEM)


def select(chooser, x):
    high = x.astype(bf16)
    rest = x - high.astype(f32)
    mid = rest.astype(bf16)
    low = (rest - mid.astype(f32)).astype(bf16)
    terms = jnp.concatenate([high, mid, low], axis=1)
    out = lax.dot_general(chooser, terms, (((1,), (0,)), ((), ())), preferred_element_type=f32)
    n = x.shape[1]
    return out[:, :n] + out[:, n : 2 * n] + out[:, 2 * n :]


def eye():
    return lax.broadcasted_iota(jnp.int32, (128, 128), 0) == lax.broadcasted_iota(
        jnp.int32, (128, 128), 1
    )


def gather_kernel(index_ref, table_ref, out_ref):
    group = 32

    def some(step, _):
        for j in range(group):
            at = step * group + j
            out_ref[at] = table_ref[index_ref[at]]
        return 0

    lax.fori_loop(0, out_ref.shape[0] // group, some, 0)


def gather_call(index, table):
    return pl.pallas_call(
        gather_kernel,
        out_shape=jax.ShapeDtypeStruct(index.shape + table.shape[1:], table.dtype),
        in_specs=[SMEM, VMEM],
        out_specs=VMEM,
        compiler_params=params(),
    )(index, table)


def finish_score(v_ref, ms_ref, pace, sums, tops, highest):
    rows = v_ref.shape[0]
    chunks = rows // 128
    ms_ref[0:chunks, :] = jnp.zeros((chunks, 128), f32)

    @pl.when(jnp.logical_not(highest < SAFE))
    def _():
        lane = lax.broadcasted_iota(jnp.int32, (8, 128), 1)

        def body(step, _):
            at = pl.ds(pl.multiple_of(step * 8, 8), 8)
            t = v_ref[at, :] * pace[...]
            m = jnp.max(t, axis=1, keepdims=True)
            total = jnp.sum(jnp.exp2(t - m), axis=1, keepdims=True)
            tops[at, :] = jnp.broadcast_to(m, (8, 128))
            sums[at, :] = jnp.where(lane == 0, total, 0.0)
            return 0

        lax.fori_loop(0, rows // 8, body, 0)
        for c in range(chunks):
            ms_ref[c : c + 1, :] = jnp.sum(
                jnp.where(eye(), tops[c * 128 : (c + 1) * 128, :], 0.0), axis=0, keepdims=True
            )

    total = lax.dot_general(
        jnp.ones((8, 128), f32), sums[...], (((1,), (1,)), ((), ())), precision=HI, preferred_element_type=f32
    )
    for c in range(chunks):
        ms_ref[chunks + c : chunks + c + 1, :] = total[0:1, c * 128 : (c + 1) * 128]


def values_kernel(blocks, x_ref, y_ref, v_ref, ms_ref, wide, yt, pace, sums, tops):
    half = BLOCK // 2
    wide[...] = y_ref[...].astype(f32)
    for k in range(blocks):
        for side in range(2):
            at = k * BLOCK + side * half
            yt[at : at + half, :] = wide[pl.ds(2 * k + side, half, stride=2 * blocks), :].astype(bf16)
    tile_c = 1024
    tiles = v_ref.shape[1] // tile_c
    sums[...] = jnp.zeros(sums.shape, f32)

    def product(step):
        cols = pl.ds(pl.multiple_of(step * tile_c, tile_c), tile_c)
        return cols, lax.dot_general(
            x_ref[...], yt[cols, :], (((1,), (1,)), ((), ())), preferred_element_type=f32
        )

    def tile(step, _):
        cols, s = product(step)
        grown = 1.0 + jnp.exp2(s * LOG2E)
        v_ref[:, cols] = jnp.log(grown)
        e = grown * grown
        part = e[:, 0:128]
        for k in range(1, tile_c // 128):
            part = part + e[:, k * 128 : (k + 1) * 128]
        sums[...] += part
        return 0

    lax.fori_loop(0, tiles, tile, 0)
    highest = jnp.max(sums[...])

    @pl.when(jnp.logical_not(highest < SAFE))
    def _():
        def again(step, _):
            cols, s = product(step)
            v_ref[:, cols] = jnp.maximum(s, 0.0) + jnp.log(1.0 + jnp.exp2(jnp.abs(s) * -LOG2E))
            return 0

        lax.fori_loop(0, tiles, again, 0)
        pace[...] = jnp.full(pace.shape, SCALE, f32)

    finish_score(v_ref, ms_ref, pace, sums, tops, highest)


def score_scratch(rows, width):
    return [pltpu.VMEM((8, width), f32), pltpu.VMEM((rows, 128), f32), pltpu.VMEM((rows, 128), f32)]


def values_call(x, y, blocks):
    rows, width = x.shape[0], blocks * BLOCK
    return pl.pallas_call(
        functools.partial(values_kernel, blocks),
        out_shape=[
            pltpu.VMEM((rows, width), f32),
            jax.ShapeDtypeStruct((rows // 64, 128), f32),
        ],
        in_specs=[VMEM, VMEM],
        out_specs=[VMEM] * 2,
        scratch_shapes=[pltpu.VMEM(y.shape, f32), pltpu.VMEM(y.shape, bf16)] + score_scratch(rows, width),
        compiler_params=params(),
    )(x, y)


def score(v_ref, ms_ref, pace, sums, tops):
    rows, width = v_ref.shape
    step_rows = 128

    def body(step, highest):
        base = pl.multiple_of(step * step_rows, step_rows)
        total = [None] * (step_rows // 8)
        for k in range(width // 128):
            cols = slice(k * 128, (k + 1) * 128)
            scale = pace[:, cols]
            for part in range(step_rows // 8):
                e = jnp.exp2(v_ref[pl.ds(base + part * 8, 8), cols] * scale)
                total[part] = e if k == 0 else total[part] + e
        for part in range(step_rows // 8):
            sums[pl.ds(base + part * 8, 8), :] = total[part]
            highest = jnp.maximum(highest, total[part])
        return highest

    highest = lax.fori_loop(0, rows // step_rows, body, jnp.zeros((8, 128), f32))
    finish_score(v_ref, ms_ref, pace, sums, tops, jnp.max(highest))


def pace_step(pace, util, limit):
    return jnp.sqrt(pace * jnp.minimum(limit / jnp.maximum(util, util_floor), pacing_cap))


def spread_pace(p, pace):
    for k in range(p.shape[0]):
        pace[:, k * BLOCK : (k + 1) * BLOCK] = jnp.broadcast_to(p[k : k + 1, :] * SCALE, (8, BLOCK))


def second_score_kernel(util_ref, recv_ref, pick_ref, v_in, v_ref, ms_ref, p_ref, limit_ref, pace, sums, tops):
    blocks = util_ref.shape[0]
    got = select(pick_ref[...], recv_ref[...].reshape(-1, BLOCK))
    limit = got[blocks:, :]
    p = pace_step(jnp.ones(limit.shape, f32), util_ref[...] + got[:blocks, :], limit)
    p_ref[...] = p
    limit_ref[...] = limit
    spread_pace(p, pace)
    score(v_in, ms_ref, pace, sums, tops)


def score_kernel(util_ref, recv_ref, pick_ref, limit_ref, old_ref, v_in, v_ref, ms_ref, p_ref, pace, sums, tops):
    util = util_ref[...] + select(pick_ref[...], recv_ref[...].reshape(-1, BLOCK))
    p = pace_step(old_ref[...], util, limit_ref[...])
    p_ref[...] = p
    spread_pace(p, pace)
    score(v_in, ms_ref, pace, sums, tops)


def score_call(kernel, v, args, outs):
    rows, width = v.shape
    small = jax.ShapeDtypeStruct((width // BLOCK, BLOCK), f32)
    return pl.pallas_call(
        kernel,
        out_shape=[pltpu.VMEM((rows, width), f32), jax.ShapeDtypeStruct((rows // 64, 128), f32)]
        + [small] * outs,
        in_specs=[VMEM] * (len(args) + 1),
        out_specs=[VMEM] * (2 + outs),
        scratch_shapes=score_scratch(rows, width),
        input_output_aliases={len(args): 0},
        compiler_params=params(),
    )(*args, pinned(v))


def combine(ms_refs):
    chunks = ms_refs[0].shape[0] // 2
    top = functools.reduce(jnp.maximum, [ref[0:chunks, :] for ref in ms_refs])
    total = sum(ref[chunks:, :] * jnp.exp2(ref[0:chunks, :] - top) for ref in ms_refs)
    return top + LOG2E * jnp.log(total)


def utility(lse, v_ref, util_ref, pace, column):
    rows, width = v_ref.shape
    for c in range(rows // 128):
        column[c * 128 : (c + 1) * 128, :] = jnp.transpose(jnp.broadcast_to(lse[c : c + 1, :], (128, 128)))
    blocks = width // BLOCK
    step_rows = 128

    def body(step, _):
        base = pl.multiple_of(step * step_rows, step_rows)
        for k in range(blocks):
            cols = slice(k * BLOCK, (k + 1) * BLOCK)
            scale = pace[:, cols]
            acc = None
            for part in range(step_rows // 8):
                at = pl.ds(base + part * 8, 8)
                v = v_ref[at, cols]
                term = jnp.exp2(v * scale - column[at, :]) * v
                acc = term if acc is None else acc + term
            util_ref[k : k + 1, :] += jnp.sum(acc, axis=0, keepdims=True)
        return 0

    util_ref[0:blocks, :] = jnp.zeros((blocks, BLOCK), f32)
    lax.fori_loop(0, rows // step_rows, body, 0)


def utility_kernel(columns, first, *refs):
    ms_refs, refs = refs[:columns], refs[columns:]
    if first:
        put_ref, own_put_ref, limit_ref, v_in, v_ref, util_ref, send_ref, pace, column = refs
        pace[...] = jnp.full(pace.shape, SCALE, f32)
    else:
        put_ref, p_ref, v_in, v_ref, util_ref, send_ref, pace, column = refs
        spread_pace(p_ref[...], pace)
    utility(combine(ms_refs), v_in, util_ref, pace, column)
    send = select(put_ref[...], util_ref[...])
    if first:
        send = send + select(own_put_ref[...], limit_ref[...])
    send_ref[...] = send.reshape(send_ref.shape)


def last_utility_kernel(columns, *refs):
    ms_refs, refs = refs[:columns], refs[columns:]
    put_ref, p_ref, v_in, v_ref, both_ref, send_ref, price_ref, pace, column = refs
    lse = combine(ms_refs)
    price_ref[...] = lse * (softness_level * LN2)
    blocks = p_ref.shape[0]
    spread_pace(p_ref[...], pace)
    utility(lse, v_in, both_ref, pace, column)
    both_ref[blocks:, :] = p_ref[...]
    send_ref[...] = select(put_ref[...], both_ref[...]).reshape(send_ref.shape)


def utility_call(kernel, v, args, util_rows, send_shape, price):
    rows, width = v.shape
    outs = [
        pltpu.VMEM((rows, width), f32),
        jax.ShapeDtypeStruct((util_rows, BLOCK), f32),
        jax.ShapeDtypeStruct(send_shape, f32),
    ]
    if price:
        outs.append(jax.ShapeDtypeStruct((rows // 128, 128), f32))
    return pl.pallas_call(
        kernel,
        out_shape=outs,
        in_specs=[VMEM] * (len(args) + 1),
        out_specs=[VMEM] * len(outs),
        scratch_shapes=[pltpu.VMEM((8, width), f32), pltpu.VMEM((rows, 128), f32)],
        input_output_aliases={len(args): 0},
        compiler_params=params(),
    )(*args, pinned(v))


def last_pace_kernel(recv_ref, back_ref, limit_ref, out_ref):
    limit = limit_ref[...]
    own = limit.shape[0]
    back = back_ref[...]
    got = select(back, recv_ref[...].reshape(-1, BLOCK))
    count = jnp.sum(back[own:, :].astype(f32), axis=1, keepdims=True)
    lone = jnp.ones(limit.shape, f32)
    for _ in range(ROUNDS - 1):
        lone = pace_step(lone, jnp.zeros(limit.shape, f32), limit)
    pace = jnp.where(count > 0.0, got[own:, :] / jnp.maximum(count, 1.0), lone)
    out_ref[...] = pace_step(pace, got[:own, :], limit)


def before(flags, axis):
    size = flags.shape[axis]
    order = jnp.arange(size)
    less = (order[:, None] < order[None, :]).astype(f32)
    moved = jnp.moveaxis(flags, axis, -1).astype(f32)
    return jnp.moveaxis(jnp.dot(moved, less), -1, axis).astype(jnp.int32)


def swap(x, axis):
    return lax.all_to_all(x, axis, split_axis=0, concat_axis=0, tiled=True)


def share_plan(equal, placed, back, shared):
    owners = equal.shape[0]
    gives = jnp.any(equal, axis=1)
    takes = jnp.any(equal, axis=2)
    slot = jnp.arange(shared, dtype=jnp.int32)[None, :, None]
    put = ((before(gives, 1)[:, None, :] == slot) & gives[:, None, :]).astype(f32)
    take_slot = ((before(takes, 1)[:, None, :] == slot) & takes[:, None, :]).astype(f32)
    pick = jnp.einsum("isk,ikw->isw", take_slot, equal.astype(f32))
    slots = shared + CAP

    def pad(x, low, high):
        return jnp.pad(x.astype(bf16), ((0, 0), (low, high), (0, 0))).reshape(owners * slots, x.shape[2])

    put, pick = pad(put, 0, CAP), pad(pick, 0, CAP).T
    own_put, limit_pick = pad(back, shared, 0), pad(placed, shared, 0).T
    return put, pick, own_put, jnp.concatenate([pick, limit_pick], axis=0)


def rounds(columns, shared, imp_vectors, mine, limits, plan, last_put, last_back):
    put, pick, own_put, first_pick = plan
    size = put.shape[1]
    owners = put.shape[0] // (shared + CAP)
    shape = (owners, shared + CAP, BLOCK)

    def everywhere(ms):
        shifts = sorted(range(1, columns), key=lambda d: -min(d, columns - d))
        return [ms] + [
            lax.ppermute(ms, "ad", [(i, (i + d) % columns) for i in range(columns)]) for d in shifts
        ]

    v, ms = values_call(imp_vectors, mine, size)
    v, util, send = utility_call(
        functools.partial(utility_kernel, columns, True),
        v, everywhere(ms) + [put, own_put, limits], size, shape, False,
    )
    recv = swap(send, "imp")
    v, ms, pace, wanted_limits = score_call(second_score_kernel, v, [util, recv, first_pick], 2)
    for step in range(2, ROUNDS):
        v, util, send = utility_call(
            functools.partial(utility_kernel, columns, False), v, everywhere(ms) + [put, pace], size, shape, False
        )
        recv = swap(send, "imp")
        v, ms, pace = score_call(score_kernel, v, [util, recv, pick, wanted_limits, pace], 1)
    _, _, send, prices = utility_call(
        functools.partial(last_utility_kernel, columns),
        v, everywhere(ms) + [last_put, pace], 2 * size, (owners, 2 * CAP, BLOCK), True,
    )
    recv = swap(send, "imp")
    final = pl.pallas_call(
        last_pace_kernel,
        out_shape=jax.ShapeDtypeStruct(limits.shape, f32),
        in_specs=[VMEM] * 3,
        out_specs=VMEM,
        compiler_params=params(),
    )(recv, last_back, limits)
    return final, prices


def per_device(imp_vectors, ad_vectors, spend_limits, targets):
    owners = lax.axis_size("imp")
    columns = lax.axis_size("ad")
    me = lax.axis_index("imp")
    emb = imp_vectors.shape[1]
    own_blocks = ad_vectors.shape[0] // BLOCK
    wanted = targets.reshape(-1)
    size = wanted.shape[0]
    limits = spend_limits.reshape(own_blocks, BLOCK)
    half = BLOCK // 2

    lists = swap(jnp.broadcast_to(wanted[None, :], (owners, size)), "imp")
    pieces = ad_vectors.reshape(own_blocks, 2, half, emb).transpose(2, 0, 1, 3)
    table = swap(pieces, "imp").reshape(owners * own_blocks, 2, emb)
    chosen = gather_call(lists.reshape(-1), table).reshape(owners, size, 2, emb)
    mine = swap(chosen, "imp").reshape(owners * size * 2, emb)

    peer = jnp.arange(owners, dtype=jnp.int32)
    equal = (lists[:, :, None] == wanted[None, None, :]) & (peer != me)[:, None, None]
    owner_of = wanted // own_blocks
    rank_of = jnp.sum(
        (owner_of[:, None] == owner_of[None, :]) & (jnp.arange(size)[None, :] < jnp.arange(size)[:, None]),
        axis=1,
    )
    lane = jnp.arange(CAP, dtype=jnp.int32)
    placed = (
        (owner_of[None, None, :] == peer[:, None, None]) & (rank_of[None, None, :] == lane[None, :, None])
    ).astype(f32)
    at_me = lists // own_blocks == me
    asked = (before(at_me, 1)[:, None, :] == lane[None, :, None]) & at_me[:, None, :]
    local = jnp.arange(own_blocks, dtype=jnp.int32)
    here = (lists[:, :, None] - me * own_blocks) == local[None, None, :]
    back = jnp.einsum("irk,ikl->irl", asked.astype(f32), here.astype(f32))

    def doubled(x):
        none = jnp.zeros_like(x)
        both = jnp.concatenate(
            [jnp.concatenate([x, none], axis=2), jnp.concatenate([none, x], axis=2)], axis=1
        )
        return both.reshape(owners * 2 * CAP, 2 * x.shape[2]).astype(bf16)

    last_put, last_back = doubled(placed), doubled(back).T
    narrow = share_plan(equal, placed, back, SHARED)

    holds = jnp.any(
        lists[:, :, None] == jnp.arange(owners * own_blocks, dtype=jnp.int32)[None, None, :], axis=1
    ).astype(bf16)
    common = lax.dot_general(holds, holds, (((1,), (1,)), ((), ())), preferred_element_type=f32)
    crowded = jnp.any((common > SHARED + 0.5) & (peer[:, None] != peer[None, :]))
    over = lax.pmax(crowded.astype(f32), "ad")
    mine, narrow, last_put, last_back, over = lax.optimization_barrier(
        (mine, narrow, last_put, last_back, over)
    )

    final, prices = rounds(columns, SHARED, imp_vectors, mine, limits, narrow, last_put, last_back)

    def take_wide():
        plan = share_plan(equal, placed, back, size)
        return rounds(columns, size, imp_vectors, mine, limits, plan, last_put, last_back)

    final, prices = lax.cond(over > 0.5, take_wide, lambda: (final, prices))
    return final.reshape(-1), prices.reshape(-1)


def solution(mesh):
    return jax.shard_map(
        per_device,
        mesh=mesh,
        in_specs=(P("imp", None), P(("imp", "ad"), None), P(("imp", "ad")), P("imp", "ad", None)),
        out_specs=(P(("imp", "ad")), P("imp")),
        check_vma=False,
    )
```

time: 394 us -> 358 us (0.909)
  blocking collectives: 119 us -> 67.9 us
  starting transfers between devices: 27 us -> 49.3 us
  waiting for transfers between devices: 40.2 us -> 58.4 us
  Pallas kernels: 160 us -> 148 us
  loops' own time: 9.25 us -> 1.03 us
  local copies, waits for them, and re-layouts: 13.6 us -> 7.7 us
    all_to_all x8 -> x3, blocking collectives: 109 us -> 58.1 us  [swap(): return lax.all_to_all(x, axis, split_axis=0, concat_axis=0, tiled=True)]
    ppermute x0 -> x12, starting transfers between devices: none -> 16.6 us  [everywhere(): lax.ppermute(ms, 'ad', [(i, (i + d) % columns) for i in range(columns)])]
    pallas_call x8, Pallas kernels: 120 us -> 108 us  [the longest x3 89.6 us: score_call(): pl.pallas_call(kernel, out_shape=[pltpu.VMEM((rows, width), f32), jax.Sha...]
    all_to_all x3 -> x4, waiting for transfers between devices: 40.2 us -> 51.4 us  [swap(): return lax.all_to_all(x, axis, split_axis=0, concat_axis=0, tiled=True)]
    gather x1 -> x0, local copies, waits for them, and re-layouts: 8.98 us -> none  [per_device(): chosen = table[lists.reshape(-1)].reshape(owners, size, 2 * emb)]
    another operation x1, loops' own time: 9.25 us -> 1.03 us  [per_device(): final, prices = lax.cond(over > 0.5, take_wide, lambda: (final, prices))]
    ppermute x0 -> x12, waiting for transfers between devices: none -> 7.02 us  [everywhere(): lax.ppermute(ms, 'ad', [(i, (i + d) % columns) for i in range(columns)])]
    all_to_all x3 -> x4, starting transfers between devices: 27 us -> 32.7 us  [swap(): return lax.all_to_all(x, axis, split_axis=0, concat_axis=0, tiled=True)]
  transfers between devices with their start and end apart: 3 -> 16, of which waited for: 3 -> 13; matrix products, arithmetic and copies ran while one was open for 5% -> 7% of each run, Pallas kernels for 1% -> 0%
where the time goes in v3:
time: 358 us; the launch traced here: 354 us
  Pallas kernels  148 us (41%)
  blocking collectives  67.9 us (19%)
  waiting for transfers between devices  58.4 us (16%)
  starting transfers between devices  49.3 us (14%)
  other arithmetic  16.3 us (5%)
  local copies, waits for them, and re-layouts  7.7 us (2%)
    pallas_call x3, Pallas kernels, score_call(): pl.pallas_call(kernel, out_shape=[pltpu.VMEM((rows, width), f32), jax.Sha...  89.6 us
    all_to_all x3, blocking collectives, swap(): return lax.all_to_all(x, axis, split_axis=0, concat_axis=0, tiled=True)  58.1 us
    all_to_all x4, waiting for transfers between devices, swap(): return lax.all_to_all(x, axis, split_axis=0, concat_axis=0, tiled=True)  51.4 us
    pallas_call x1, Pallas kernels, values_call(): pl.pallas_call(functools.partial(values_kernel, blocks), out_shape=[pltpu...  39.5 us
    all_to_all x4, starting transfers between devices, swap(): return lax.all_to_all(x, axis, split_axis=0, concat_axis=0, tiled=True)  32.7 us
    ppermute x12, starting transfers between devices, everywhere(): lax.ppermute(ms, 'ad', [(i, (i + d) % columns) for i in range(columns)])  16.6 us
    pallas_call x4, Pallas kernels, utility_call(): pl.pallas_call(kernel, out_shape=outs, in_specs=[VMEM] * (len(args) + 1),...  14.8 us
    reduce_or x1, other arithmetic, per_device(): jnp.any(lists[:, :, None] == jnp.arange(owners * own_blocks, dtype=jnp.in...  11 us
  transfers between devices with their start and end apart: 16, of which 13 were waited for; matrix products, arithmetic and copies ran while one was open for 7% of the time, Pallas kernels for 0%

profile of v3, /device:TPU:1, one launch (start us, length us, event | category | flops | bytes accessed | tf_op | source)
XLA Modules:
  0.0 354.2 jit_solution(16475185176508502482)
XLA Ops:
  2.0 13.2 %all-to-all-start.4 = ((s32[64,1,32]{2,1,0:T(1,128)}), s32[64,1,32]{2,1,0:T(1,128)S(1)}, u32[]{:S(2)}, u32[]{:S(2)}) async-start(s32[64,1,32]{2,1,0:T(1,128)} %broadcast_in_dim.2), calls=%async_computation.4 | async-start | bytes 65536 | tf_op jit(solution)/shard_map/all_to_all | solution.py:338
  15.1 4.2 %copy.111 = bf16[48,2,64,128]{3,1,0,2:T(2,128)(2,1)} copy(bf16[48,2,64,128]{3,2,1,0:T(8,128)(2,1)} %bitcast.57) | data formatting | bytes 3145728 | tf_op jit(solution)/shard_map/reshape | solution.py:411
  19.3 5.1 %all-to-all-done.4 = s32[64,1,32]{2,1,0:T(1,128)S(1)} async-done(((s32[64,1,32]{2,1,0:T(1,128)}), s32[64,1,32]{2,1,0:T(1,128)S(1)}, u32[]{:S(2)}, u32[]{:S(2)}) %all-to-all-start.4) | async-done | bytes 8224 | tf_op jit(solution)/shard_map/all_to_all | solution.py:338
  24.4 6.0 %all-to-all-start.5 = ((bf16[64,48,2,128]{3,2,1,0:T(2,128)(2,1)}), bf16[64,48,2,128]{3,2,1,0:T(2,128)(2,1)S(1)}, u32[]{:S(2)}, u32[]{:S(2)}) async-start(bf16[64,48,2,128]{3,2,1,0:T(2,128)(2,1)} %bitcast.46), calls=%async_computation.5 | async-start | bytes 3145728 | tf_op jit(solution)/shard_map/all_to_all | solution.py:338
  32.2 11.0 %fusion.5 = pred[64,3072]{1,0:T(8,128)(4,1)S(1)} fusion(s32[64,32]{1,0:T(8,128)S(1)} %bitcast.58), kind=kLoop, calls=%fused_computation.13 | loop fusion | flops 12386304 | bytes 204800 | tf_op jit(solution)/shard_map/reduce_or | solution.py:443
  44.9 9.8 %pmax.7 = f32[]{:T(128)} all-reduce(f32[]{:T(128)S(6)} %convert_element_type.108), channel_id=1, replica_groups=mesh['imp'=64,'ad'=4] {'ad'}, use_global_device_ids=true, to_apply=%region_5.6 | all-reduce | flops 1 | bytes 8 | tf_op jit(solution)/shard_map/pmax | solution.py:448
  58.3 11.8 %all-to-all-done.5 = bf16[64,48,2,128]{3,2,1,0:T(2,128)(2,1)S(1)} async-done(((bf16[64,48,2,128]{3,2,1,0:T(2,128)(2,1)}), bf16[64,48,2,128]{3,2,1,0:T(2,128)(2,1)S(1)}, u32[]{:S(2)}, u32[]{:S(2)}) %all-to-all-start.5) | async-done | bytes 1572896 | tf_op jit(solution)/shard_map/all_to_all | solution.py:338
  70.0 3.6 %shard_map.62 = bf16[2048,2,128]{2,1,0:T(2,128)(2,1)} custom-call(s32[2048]{0:T(1024)S(1)} %reshape.175.index_ref, bf16[3072,2,128]{2,1,0:T(2,128)(2,1)S(1)} %bitcast.48), custom_call_target="tpu_custom_call" | custom-call | tf_op jit(solution)/shard_map/pallas_call | solution.py:69
  73.6 6.1 %all-to-all-start.6 = ((bf16[64,32,2,128]{3,2,1,0:T(2,128)(2,1)}), bf16[64,32,2,128]{3,2,1,0:T(2,128)(2,1)S(1)}, u32[]{:S(2)}, u32[]{:S(2)}) async-start(bf16[64,32,2,128]{3,2,1,0:T(2,128)(2,1)} %bitcast.6), calls=%async_computation.6 | async-start | bytes 2097152 | tf_op jit(solution)/shard_map/all_to_all | solution.py:338
  83.4 24.9 %all-to-all-done.6 = bf16[64,32,2,128]{3,2,1,0:T(2,128)(2,1)S(1)} async-done(((bf16[64,32,2,128]{3,2,1,0:T(2,128)(2,1)}), bf16[64,32,2,128]{3,2,1,0:T(2,128)(2,1)S(1)}, u32[]{:S(2)}, u32[]{:S(2)}) %all-to-all-start.6) | async-done | bytes 1048608 | tf_op jit(solution)/shard_map/all_to_all | solution.py:338
  108.3 39.5 %shard_map.63 = (f32[1024,4096]{1,0:T(8,128)S(1)}, f32[16,128]{1,0:T(8,128)S(1)}) custom-call(bf16[1024,128]{1,0:T(8,128)(2,1)S(1)} %copy-done.4, bf16[4096,128]{1,0:T(8,128)(2,1)S(1)} %bitcast.55), custom_call_target="tpu_custom_call" | custom-call | tf_op jit(solution)/shard_map/pallas_call | solution.py:159
  147.8 2.8 collective-permute-start.12
  154.3 3.6 %shard_map.64 = (f32[1024,4096]{1,0:T(8,128)S(1)}, f32[32,128]{1,0:T(8,128)S(1)}, f32[64,8,128]{2,1,0:T(8,128)S(1)}) custom-call(f32[16,128]{1,0:T(8,128)S(1)} %get-tuple-element.92.refs_0_, f32[16,128]{1,0:T(8,128)S(1)} %collective-permute-done.12.refs_1_, f32[16,128]{1,0:T(8,128)S(1)} %collective-permute-done.13.refs_2_, ...), custom_call_target="tpu_custom_call", output_to_operand_aliasing={{0}: (7, {})} | custom-call | tf_op jit(solution)/shard_map/pallas_call | solution.py:305
  158.0 19.6 %all_to_all.55.recv_ref = f32[64,8,128]{2,1,0:T(8,128)S(1)} all-to-all(f32[64,8,128]{2,1,0:T(8,128)S(1)} %get-tuple-element.97), channel_id=1, replica_groups=mesh['imp'=64,'ad'=4] {'imp'}, dimensions={0} | all-to-all | bytes 524288 | tf_op jit(solution)/shard_map/all_to_all | solution.py:338
  177.6 29.9 %shard_map.65 = (f32[1024,4096]{1,0:T(8,128)S(1)}, f32[16,128]{1,0:T(8,128)S(1)}, f32[32,128]{1,0:T(8,128)S(1)}, f32[32,128]{1,0:T(8,128)S(1)}) custom-call(f32[32,128]{1,0:T(8,128)S(1)} %get-tuple-element.96.util_ref, f32[64,8,128]{2,1,0:T(8,128)S(1)} %all_to_all.55.recv_ref, ...), custom_call_target="tpu_custom_call", output_to_operand_aliasing={{0}: (3, {})} | custom-call | tf_op jit(solution)/shard_map/pallas_call | solution.py:225
  213.8 3.5 shard_map.66
  217.3 19.2 %all_to_all.56.recv_ref = f32[64,8,128]{2,1,0:T(8,128)S(1)} all-to-all(f32[64,8,128]{2,1,0:T(8,128)S(1)} %get-tuple-element.104), channel_id=1, replica_groups=mesh['imp'=64,'ad'=4] {'imp'}, dimensions={0} | all-to-all | bytes 524288 | tf_op jit(solution)/shard_map/all_to_all | solution.py:338
  236.6 29.9 %shard_map.67 = (f32[1024,4096]{1,0:T(8,128)S(1)}, f32[16,128]{1,0:T(8,128)S(1)}, f32[32,128]{1,0:T(8,128)S(1)}) custom-call(f32[32,128]{1,0:T(8,128)S(1)} %get-tuple-element.103.util_ref, f32[64,8,128]{2,1,0:T(8,128)S(1)} %all_to_all.56.recv_ref, bf16[32,512]{1,0:T(8,128)(2,1)S(1)} %bitcast.53, ...), custom_call_target="tpu_custom_call", output_to_operand_aliasing={{0}: (5, {})} | custom-call | tf_op jit(solution)/shard_map/pallas_call | solution.py:225
  271.4 3.5 shard_map.68
  274.9 19.2 %all_to_all.57.recv_ref = f32[64,8,128]{2,1,0:T(8,128)S(1)} all-to-all(f32[64,8,128]{2,1,0:T(8,128)S(1)} %get-tuple-element.112), channel_id=1, replica_groups=mesh['imp'=64,'ad'=4] {'imp'}, dimensions={0} | all-to-all | bytes 524288 | tf_op jit(solution)/shard_map/all_to_all | solution.py:338
  294.1 29.9 %shard_map.69 = (f32[1024,4096]{1,0:T(8,128)S(1)}, f32[16,128]{1,0:T(8,128)S(1)}, f32[32,128]{1,0:T(8,128)S(1)}) custom-call(f32[32,128]{1,0:T(8,128)S(1)} %get-tuple-element.111.util_ref, f32[64,8,128]{2,1,0:T(8,128)S(1)} %all_to_all.57.recv_ref, bf16[32,512]{1,0:T(8,128)(2,1)S(1)} %bitcast.54, ...), custom_call_target="tpu_custom_call", output_to_operand_aliasing={{0}: (5, {})} | custom-call | tf_op jit(solution)/shard_map/pallas_call | solution.py:225
  329.9 4.1 %shard_map.70 = (f32[1024,4096]{1,0:T(8,128)S(1)}, f32[64,128]{1,0:T(8,128)}, f32[64,4,128]{2,1,0:T(4,128)}, f32[8,128]{1,0:T(8,128)}) custom-call(f32[16,128]{1,0:T(8,128)S(1)} %get-tuple-element.114.refs_0_, f32[16,128]{1,0:T(8,128)S(1)} %collective-permute-done.21.refs_1_, ...), custom_call_target="tpu_custom_call", output_to_operand_aliasing={{0}: (6, {})} | custom-call | tf_op jit(solution)/shard_map/pallas_call | solution.py:305
  334.0 7.4 %all-to-all-start.10 = ((f32[64,4,128]{2,1,0:T(4,128)}), f32[64,4,128]{2,1,0:T(4,128)S(1)}, u32[]{:S(2)}, u32[]{:S(2)}) async-start(f32[64,4,128]{2,1,0:T(4,128)} %get-tuple-element.118), calls=%async_computation.10 | async-start | bytes 262144 | tf_op jit(solution)/shard_map/all_to_all | solution.py:338
  342.2 9.7 %all-to-all-done.10.recv_ref = f32[64,4,128]{2,1,0:T(4,128)S(1)} async-done(((f32[64,4,128]{2,1,0:T(4,128)}), f32[64,4,128]{2,1,0:T(4,128)S(1)}, u32[]{:S(2)}, u32[]{:S(2)}) %all-to-all-start.10) | async-done | bytes 131104 | tf_op jit(solution)/shard_map/all_to_all | solution.py:338
  (71 shorter events, 34.0 us)
Async XLA Ops:
  0.6 107.7 %copy-start.4 = (bf16[1024,128]{1,0:T(8,128)(2,1)S(1)}, bf16[1024,128]{1,0:T(8,128)(2,1)}, u32[]{:S(2)}) copy-start(bf16[1024,128]{1,0:T(8,128)(2,1)} %x_ref.1) | copy-start | bytes 786436
  0.6 153.7 %copy-start.7 = (f32[6144]{0:T(1024)S(1)}, f32[6144]{0:T(1024)}, u32[]{:S(2)}) copy-start(f32[6144]{0:T(1024)} %param.8) | copy-start | bytes 73732
  2.0 22.4 %all-to-all-start.4 = ((s32[64,1,32]{2,1,0:T(1,128)}), s32[64,1,32]{2,1,0:T(1,128)S(1)}, u32[]{:S(2)}, u32[]{:S(2)}) async-start(s32[64,1,32]{2,1,0:T(1,128)} %broadcast_in_dim.2), calls=%async_computation.4 | async-start | bytes 65536 | tf_op jit(solution)/shard_map/all_to_all | solution.py:338
  24.4 45.6 %all-to-all-start.5 = ((bf16[64,48,2,128]{3,2,1,0:T(2,128)(2,1)}), bf16[64,48,2,128]{3,2,1,0:T(2,128)(2,1)S(1)}, u32[]{:S(2)}, u32[]{:S(2)}) async-start(bf16[64,48,2,128]{3,2,1,0:T(2,128)(2,1)} %bitcast.46), calls=%async_computation.5 | async-start | bytes 3145728 | tf_op jit(solution)/shard_map/all_to_all | solution.py:338
  56.6 25.8 %copy-start.8 = (pred[64,32]{1,0:T(8,128)(4,1)}, pred[64,32]{1,0:T(8,128)(4,1)S(1)}, u32[]{:S(2)}) copy-start(pred[64,32]{1,0:T(8,128)(4,1)S(1)} %get-tuple-element.158) | copy-start | bytes 6148
  73.6 34.7 %all-to-all-start.6 = ((bf16[64,32,2,128]{3,2,1,0:T(2,128)(2,1)}), bf16[64,32,2,128]{3,2,1,0:T(2,128)(2,1)S(1)}, u32[]{:S(2)}, u32[]{:S(2)}) async-start(bf16[64,32,2,128]{3,2,1,0:T(2,128)(2,1)} %bitcast.6), calls=%async_computation.6 | async-start | bytes 2097152 | tf_op jit(solution)/shard_map/all_to_all | solution.py:338
  147.8 5.5 %collective-permute-start.12 = (f32[16,128]{1,0:T(8,128)S(1)}, f32[16,128]{1,0:T(8,128)S(1)}, u32[]{:S(2)}, u32[]{:S(2)}) collective-permute-start(f32[16,128]{1,0:T(8,128)S(1)} %get-tuple-element.92.refs_0_), channel_id=1, source_target_pairs={{0,2},{1,3},{2,0},{3,1},{4,6},{5,7},{6,4},{7,5},{8,10},{9,11},{10,... | collective-permute-start | bytes 24584 | tf_op jit(solution)/shard_map/ppermute | solution.py:368
  150.6 3.7 %collective-permute-start.13 = (f32[16,128]{1,0:T(8,128)S(1)}, f32[16,128]{1,0:T(8,128)S(1)}, u32[]{:S(2)}, u32[]{:S(2)}) collective-permute-start(f32[16,128]{1,0:T(8,128)S(1)} %get-tuple-element.92.refs_0_), channel_id=1, source_target_pairs={{0,1},{1,2},{2,3},{3,0},{4,5},{5,6},{6,7},{7,4},{8,9},{9,10},{10,1... | collective-permute-start | bytes 24584 | tf_op jit(solution)/shard_map/ppermute | solution.py:368
  150.9 3.4 collective-permute-start.14
  207.4 4.0 %collective-permute-start.15 = (f32[16,128]{1,0:T(8,128)S(1)}, f32[16,128]{1,0:T(8,128)S(1)}, u32[]{:S(2)}, u32[]{:S(2)}) collective-permute-start(f32[16,128]{1,0:T(8,128)S(1)} %get-tuple-element.100.refs_0_), channel_id=1, source_target_pairs={{0,2},{1,3},{2,0},{3,1},{4,6},{5,7},{6,4},{7,5},{8,10},{9,11},{10,... | collective-permute-start | bytes 24584 | tf_op jit(solution)/shard_map/ppermute | solution.py:368
  208.6 4.0 %collective-permute-start.16 = (f32[16,128]{1,0:T(8,128)S(1)}, f32[16,128]{1,0:T(8,128)S(1)}, u32[]{:S(2)}, u32[]{:S(2)}) collective-permute-start(f32[16,128]{1,0:T(8,128)S(1)} %get-tuple-element.100.refs_0_), channel_id=1, source_target_pairs={{0,1},{1,2},{2,3},{3,0},{4,5},{5,6},{6,7},{7,4},{8,9},{9,10},{10,1... | collective-permute-start | bytes 24584 | tf_op jit(solution)/shard_map/ppermute | solution.py:368
  211.0 2.8 collective-permute-start.17
  266.4 4.0 %collective-permute-start.18 = (f32[16,128]{1,0:T(8,128)S(1)}, f32[16,128]{1,0:T(8,128)S(1)}, u32[]{:S(2)}, u32[]{:S(2)}) collective-permute-start(f32[16,128]{1,0:T(8,128)S(1)} %get-tuple-element.108.refs_0_), channel_id=1, source_target_pairs={{0,2},{1,3},{2,0},{3,1},{4,6},{5,7},{6,4},{7,5},{8,10},{9,11},{10,... | collective-permute-start | bytes 24584 | tf_op jit(solution)/shard_map/ppermute | solution.py:368
  266.8 3.7 %collective-permute-start.19 = (f32[16,128]{1,0:T(8,128)S(1)}, f32[16,128]{1,0:T(8,128)S(1)}, u32[]{:S(2)}, u32[]{:S(2)}) collective-permute-start(f32[16,128]{1,0:T(8,128)S(1)} %get-tuple-element.108.refs_0_), channel_id=1, source_target_pairs={{0,1},{1,2},{2,3},{3,0},{4,5},{5,6},{6,7},{7,4},{8,9},{9,10},{10,1... | collective-permute-start | bytes 24584 | tf_op jit(solution)/shard_map/ppermute | solution.py:368
  268.6 2.8 collective-permute-start.20
  324.0 4.3 %collective-permute-start.21 = (f32[16,128]{1,0:T(8,128)S(1)}, f32[16,128]{1,0:T(8,128)S(1)}, u32[]{:S(2)}, u32[]{:S(2)}) collective-permute-start(f32[16,128]{1,0:T(8,128)S(1)} %get-tuple-element.114.refs_0_), channel_id=1, source_target_pairs={{0,2},{1,3},{2,0},{3,1},{4,6},{5,7},{6,4},{7,5},{8,10},{9,11},{10,... | collective-permute-start | bytes 24584 | tf_op jit(solution)/shard_map/ppermute | solution.py:368
  325.2 4.0 %collective-permute-start.22 = (f32[16,128]{1,0:T(8,128)S(1)}, f32[16,128]{1,0:T(8,128)S(1)}, u32[]{:S(2)}, u32[]{:S(2)}) collective-permute-start(f32[16,128]{1,0:T(8,128)S(1)} %get-tuple-element.114.refs_0_), channel_id=1, source_target_pairs={{0,1},{1,2},{2,3},{3,0},{4,5},{5,6},{6,7},{7,4},{8,9},{9,10},{10,1... | collective-permute-start | bytes 24584 | tf_op jit(solution)/shard_map/ppermute | solution.py:368
  326.7 3.2 collective-permute-start.23
  334.0 17.8 %all-to-all-start.10 = ((f32[64,4,128]{2,1,0:T(4,128)}), f32[64,4,128]{2,1,0:T(4,128)S(1)}, u32[]{:S(2)}, u32[]{:S(2)}) async-start(f32[64,4,128]{2,1,0:T(4,128)} %get-tuple-element.118), calls=%async_computation.10 | async-start | bytes 262144 | tf_op jit(solution)/shard_map/all_to_all | solution.py:338
  353.1 0.6 copy-start.9
